TPU v7x, 32 devices: a whole 2x2x4 slice. The times are simulated.
32 devices in a mesh: rows: 8 (over z, y), cols: 4 (over x, core).
Axes of the slice: x: 2, y: 2, z: 4, core: 2. Of those that a mesh axis runs over, the one named last changes fastest.
Arguments:
- l_blocks: bfloat16 [256, 64, 1920], P(('rows', 'cols')), may hold values from -0.25 to 0.25
- s_blocks: bfloat16 [256, 64, 1280], P('rows', None, 'cols'), may hold values from -6 to 6
- l_index: int32 [256, 30], P(('rows', 'cols')), may hold values from 0 to 255, as said below
- s_cols: int32 [256, 20], replicated, may hold values from 0 to 255, as said below
- c_index: int32 [256, 24], P(('rows', 'cols')), may hold values from 0 to 255, as said below
Outputs:
- product: bfloat16 [256, 64, 1536], P(('rows', 'cols'))
Inputs may be any that keep to these rules, and one draw needn't show every extreme that they name: `l_index`: the 30 entries of block-row i are distinct and lie in the window of 31 block-rows starting at max(0, min(i - 15, 225)). `s_cols`: the entries of one block-row are distinct; those in slots p * 5 to (p + 1) * 5 - 1 are congruent to p modulo 20 // 5 and lie within 7 such columns around the block-row. `c_index`: the entries of one block-row are distinct; those in slots p * 6 to (p + 1) * 6 - 1 are congruent to p modulo 24 // 6 and lie within 16 such columns around the block-row.
All inputs are finite; a program needn't handle non-finite values.
Results may differ from a plain program's by a relative error of at most 0.001.
Values may be sent and summed in bfloat16 or wider, within the bound.
A program may use at most 192 MiB of HBM per device.

v0:
```python
import math

import jax
import jax.numpy as jnp
from jax import lax
from jax.sharding import PartitionSpec as P

HL = 15


def padded(block, sides, width):
    for axis, dim in sides:
        count = lax.axis_size(axis)
        forward = [(i, i + 1) for i in range(count - 1)]
        backward = [(target, source) for source, target in forward]
        low = lax.ppermute(
            lax.slice_in_dim(block, block.shape[dim] - width, None, axis=dim), axis, forward
        )
        high = lax.ppermute(lax.slice_in_dim(block, 0, width, axis=dim), axis, backward)
        block = jnp.concatenate([low, block, high], axis=dim)
    return block


def row_products(l_rows, l_ids, want_index, s_near, slot_cols, first):
    total = l_rows.shape[0]
    width = l_rows.shape[1]
    slot_total = s_near.shape[2] // width
    kept = want_index.shape[1]
    s_four = s_near.reshape(s_near.shape[0], width, slot_total, width)
    s_four = jnp.concatenate(
        [s_four, jnp.zeros((s_four.shape[0], width, 1, width), s_four.dtype)], axis=2
    )
    per_turn = math.gcd(total, max(1, 96 // kept))

    def single(left_row, left_ids, want_cols):
        slot_ids = jnp.take(slot_cols, left_ids, axis=0)
        match = slot_ids[:, None, :] == want_cols[None, :, None]
        slot_pick = jnp.sum(
            jnp.where(match, lax.iota(jnp.int32, slot_total)[None, None, :], 0),
            axis=2,
            dtype=jnp.int32,
        )
        found = jnp.any(match, axis=2)
        slot_pick = jnp.where(found, slot_pick, slot_total)
        local_ids = left_ids - first
        picked = s_four[local_ids[:, None], :, slot_pick, :]
        left_three = left_row.reshape(width, left_ids.shape[0], width)
        summed = jnp.einsum("akb,kmbc->amc", left_three, picked, preferred_element_type=jnp.float32)
        return summed.reshape(width, kept * width).astype(jnp.bfloat16)

    def one_group(group):
        return jax.vmap(single)(group[0], group[1], group[2])

    shaped = tuple(
        (
            a.reshape((total // per_turn, per_turn) + a.shape[1:])
            for a in (l_rows, l_ids, want_index)
        )
    )
    result = lax.map(one_group, shaped)
    return result.reshape((total,) + result.shape[2:])


def shards(l_blocks, s_blocks, l_index, s_cols, c_index):
    row_here = lax.axis_index("rows")
    group_size = s_blocks.shape[0]
    group_first = row_here * group_size
    whole = lax.all_gather(s_blocks, "cols", axis=2, tiled=True)
    nearby = padded(whole, (("rows", 0),), HL)
    return row_products(l_blocks, l_index, c_index, nearby, s_cols, group_first - HL)


def solution(mesh):
    return jax.shard_map(
        shards,
        mesh=mesh,
        in_specs=(
            P(("rows", "cols"), None, None),
            P("rows", None, "cols"),
            P(("rows", "cols"), None),
            P(),
            P(("rows", "cols"), None),
        ),
        out_specs=P(("rows", "cols"), None, None),
        check_vma=False,
    )
```

profile of v0, /device:TPU:19, one launch (start us, length us, event | category | flops | bytes accessed | tf_op | source)
XLA Modules:
  0.0 415.9 jit_solution(11024143103870345347)
XLA Ops:
  6.5 5.9 %copy.44 = bf16[32,64,320]{1,0,2:T(8,128)(2,1)} copy(bf16[32,64,320]{2,1,0:T(8,128)(2,1)} %param.8) | data formatting | bytes 2621440 | tf_op args[1]
  12.5 70.9 %all-gather.2.cloned.1.call-done = bf16[32,64,1280]{1,0,2:T(8,128)(2,1)} async-done(((bf16[32,64,320]{1,0,2:T(8,128)(2,1)}), bf16[32,64,1280]{1,0,2:T(8,128)(2,1)}) %all-gather.2.cloned.1.call-update) | async-done | bytes 5242896 | tf_op jit(solution)/shard_map/all_gather | solution.py:68
  83.4 9.8 %fusion.13 = (bf16[15,64,1280]{1,0,2:T(8,128)(2,1)}, bf16[15,64,1280]{1,0,2:T(8,128)(2,1)}) fusion(bf16[32,64,1280]{1,0,2:T(8,128)(2,1)} %all-gather.2.cloned.1.call-done), kind=kLoop, calls=%fused_computation.26 | loop fusion | bytes 9830400 | tf_op jit(solution)/shard_map/slice | solution.py:17
  93.2 7.1 %copy.45 = bf16[15,64,1280]{2,1,0:T(8,128)(2,1)} copy(bf16[15,64,1280]{1,0,2:T(8,128)(2,1)} %get-tuple-element.104) | data formatting | bytes 4915200 | tf_op jit(solution)/shard_map/slice | solution.py:17
  100.3 3.1 collective-permute-start
  103.4 7.1 %copy.46 = bf16[15,64,1280]{2,1,0:T(8,128)(2,1)} copy(bf16[15,64,1280]{1,0,2:T(8,128)(2,1)} %get-tuple-element.105) | data formatting | bytes 4915200 | tf_op jit(solution)/shard_map/slice | solution.py:19
  110.5 3.2 collective-permute-start.1
  113.9 12.7 %copy.47 = bf16[32,64,1280]{2,1,0:T(8,128)(2,1)} copy(bf16[32,64,1280]{1,0,2:T(8,128)(2,1)} %all-gather.2.cloned.1.call-done) | data formatting | bytes 10485760 | tf_op jit(solution)/shard_map/all_gather | solution.py:68
  126.5 82.3 %collective-permute-done = bf16[15,64,1280]{2,1,0:T(8,128)(2,1)S(1)} collective-permute-done((bf16[15,64,1280]{2,1,0:T(8,128)(2,1)}, bf16[15,64,1280]{2,1,0:T(8,128)(2,1)S(1)}, u32[]{:S(2)}, u32[]{:S(2)}) %collective-permute-start) | collective-permute-done | bytes 2457632 | tf_op jit(solution)/shard_map/ppermute | solution.py:16
  208.8 2.5 collective-permute-done.1
  211.3 8.8 %pad_maximum_fusion = bf16[62,64,1280]{2,1,0:T(8,128)(2,1)} fusion(bf16[15,64,1280]{2,1,0:T(8,128)(2,1)} %collective-permute-done.1, bf16[32,64,1280]{2,1,0:T(8,128)(2,1)} %copy.47, bf16[15,64,1280]{2,1,0:T(8,128)(2,1)S(1)} %collective-permute-done), kind=kLoop, calls=%fused_computation.25 | loop fusion | flops 10158080 | bytes 20316160 | tf_op jit(solution)/shard_map/concatenate | solution.py:20
  220.2 29.2 %reshape.109 = bf16[62,64,20,64]{3,2,1,0:T(8,128)(2,1)} reshape(bf16[62,64,1280]{2,1,0:T(8,128)(2,1)} %pad_maximum_fusion) | data formatting | bytes 20316160 | tf_op jit(solution)/shard_map/reshape | solution.py:29
  249.3 12.8 %copy.54 = bf16[62,64,20,64]{3,1,2,0:T(8,128)(2,1)S(1)} copy(bf16[62,64,20,64]{3,2,1,0:T(8,128)(2,1)} %reshape.109) | data formatting | bytes 20316160
  262.1 11.0 %concatenate.10.clone = bf16[62,64,21,64]{3,1,2,0:T(8,128)(2,1)} pad(bf16[62,64,20,64]{3,1,2,0:T(8,128)(2,1)S(1)} %copy.54, bf16[]{:T(256)} %constant.33.clone.1), padding=0_0x0_0x0_1x0_0 | pad | bytes 20824066 | tf_op jit(solution)/shard_map/concatenate | solution.py:30
  273.1 135.9 %while.10 = (s32[]{:T(128)}, bf16[2,4,64,1536]{3,2,1,0:T(8,128)(2,1)}, bf16[2,4,64,1920]{3,2,1,0:T(8,128)(2,1)}, s32[2,4,30]{2,1,0:T(4,128)S(1)}, s32[]{:T(128)}...) while((s32[]{:T(128)}, ...), condition=%wide.region_3.4_spmd, body=%wide.region_0.3_spmd.sunk | while | flops 1510650240 | bytes 81435040 | solution.py:60
  273.2 0.6 gather_fusion
  274.3 0.2 compare_reduce_fusion.2
  274.8 39.2 %gather_fusion.1 = bf16[2880,64,64]{2,1,0:T(8,128)(2,1)} fusion(bf16[62,64,21,64]{3,1,2,0:T(8,128)(2,1)} %get-tuple-element.180, s32[2880]{0:T(1024)S(1)} %reshape.142), kind=kCustom, calls=%fused_computation.1.clone.1 | custom fusion | bytes 47208960 | tf_op jit(solution)/shard_map/while/body/eval_jaxpr/vmap()/gather | solution.py:46
  314.0 1.3 constant_dynamic-slice_fusion.2
  315.2 2.1 reshape.143
  317.4 19.4 %bitcast_convert_fusion.2 = bf16[4,64,24,64]{3,1,2,0:T(8,128)(2,1)} fusion(bf16[4,30,24,64,64]{4,3,2,1,0:T(8,128)(2,1)} %bitcast.48, bf16[4,64,30,64,1]{3,2,1,0,4:T(8,128)(2,1)S(1)} %bitcast.49), kind=kOutput, calls=%fused_computation.4.clone.1 | convolution fusion | flops 1510342656 | bytes 25362432 | tf_op jit(solution)/shard_map/while/body/eval_jaxpr/vmap(akb,kmbc->amc)/dot_general | solution.py:48
  336.7 2.4 copy.74
  339.2 1.0 convert_element_type.17
  340.2 0.9 constant_dynamic-update-slice_fusion.2
  341.2 0.6 gather_fusion
  342.7 39.2 %gather_fusion.1 = bf16[2880,64,64]{2,1,0:T(8,128)(2,1)} fusion(bf16[62,64,21,64]{3,1,2,0:T(8,128)(2,1)} %get-tuple-element.180, s32[2880]{0:T(1024)S(1)} %reshape.142), kind=kCustom, calls=%fused_computation.1.clone.1 | custom fusion | bytes 47208960 | tf_op jit(solution)/shard_map/while/body/eval_jaxpr/vmap()/gather | solution.py:46
  381.9 1.3 constant_dynamic-slice_fusion.2
  383.2 2.1 reshape.143
  385.4 19.4 %bitcast_convert_fusion.2 = bf16[4,64,24,64]{3,1,2,0:T(8,128)(2,1)} fusion(bf16[4,30,24,64,64]{4,3,2,1,0:T(8,128)(2,1)} %bitcast.48, bf16[4,64,30,64,1]{3,2,1,0,4:T(8,128)(2,1)S(1)} %bitcast.49), kind=kOutput, calls=%fused_computation.4.clone.1 | convolution fusion | flops 1510342656 | bytes 25362432 | tf_op jit(solution)/shard_map/while/body/eval_jaxpr/vmap(akb,kmbc->amc)/dot_general | solution.py:48
  404.7 2.4 copy.74
  407.2 1.0 convert_element_type.17
  408.1 0.9 constant_dynamic-update-slice_fusion.2
  (39 shorter events, 1.8 us)
Async XLA Ops:
  6.5 76.8 %all-gather.2.cloned.1.call-start = ((), (), s32[]{:S(2)}) async-start(), calls=%async_computation | async-start | bytes 13107200 | tf_op jit(solution)/shard_map/all_gather | solution.py:68
  100.3 108.6 %collective-permute-start = (bf16[15,64,1280]{2,1,0:T(8,128)(2,1)}, bf16[15,64,1280]{2,1,0:T(8,128)(2,1)S(1)}, u32[]{:S(2)}, u32[]{:S(2)}) collective-permute-start(bf16[15,64,1280]{2,1,0:T(8,128)(2,1)} %copy.45), channel_id=1, source_target_pairs={{0,4},{4,8},{8,12},{12,16},{16,20},{20,24},{24,28},{1,5},{5,9},{9,... | collective-permute-start | bytes 7372808 | tf_op jit(solution)/shard_map/ppermute | solution.py:16
  103.4 10.4 %copy-start.2 = (s32[256,20]{0,1:T(8,128)S(1)}, s32[256,20]{0,1:T(8,128)}, u32[]{:S(2)}) copy-start(s32[256,20]{0,1:T(8,128)} %param.10) | copy-start | bytes 61444
  110.5 100.8 %collective-permute-start.1 = (bf16[15,64,1280]{2,1,0:T(8,128)(2,1)}, bf16[15,64,1280]{2,1,0:T(8,128)(2,1)}, u32[]{:S(2)}, u32[]{:S(2)}) collective-permute-start(bf16[15,64,1280]{2,1,0:T(8,128)(2,1)} %copy.46), channel_id=1, source_target_pairs={{4,0},{8,4},{12,8},{16,12},{20,16},{24,20},{28,24},{5,1},{9,5},{13... | collective-permute-start | bytes 7372808 | tf_op jit(solution)/shard_map/ppermute | solution.py:19
  262.1 11.0 %copy-start = (s32[8,30]{1,0:T(8,128)S(1)}, s32[8,30]{1,0:T(8,128)}, u32[]{:S(2)}) copy-start(s32[8,30]{1,0:T(8,128)} %param.9) | copy-start | bytes 2884
  262.1 11.0 %copy-start.1 = (s32[8,24]{1,0:T(8,128)S(1)}, s32[8,24]{1,0:T(8,128)}, u32[]{:S(2)}) copy-start(s32[8,24]{1,0:T(8,128)} %param.11) | copy-start | bytes 2308
Sparse Core Ops, SparseCore 0:
  12.6 70.7 all-gather.1
where the time goes:
time: 419 us; the launch traced here: 416 us
  local copies, waits for them, and re-layouts  192 us (46%)
  waiting for transfers between devices  156 us (37%)
  matrix products  38.7 us (9%)
  between operations  13.5 us (3%)
  other arithmetic  9.79 us (2%)
  starting transfers between devices  6.34 us (2%)
    ppermute x1, waiting for transfers between devices, padded(): lax.ppermute(lax.slice_in_dim(block, block.shape[dim] - width, None, axis...  82.3 us
    gather x2, local copies, waits for them, and re-layouts, single(): picked = s_four[local_ids[:, None], :, slot_pick, :]  78.4 us
    all_gather x1, waiting for transfers between devices, shards(): whole = lax.all_gather(s_blocks, 'cols', axis=2, tiled=True)  70.9 us
    dot_general x2, matrix products, single(): jnp.einsum('akb,kmbc->amc', left_three, picked, preferred_element_type=jn...  38.7 us
    reshape x1, local copies, waits for them, and re-layouts, row_products(): s_four = s_near.reshape(s_near.shape[0], width, slot_total, width)  29.2 us
    unnamed x8, local copies, waits for them, and re-layouts  18.7 us
    slice x2, local copies, waits for them, and re-layouts, padded(): lax.slice_in_dim(block, block.shape[dim] - width, None, axis=dim)  16.9 us
    all_gather x1, local copies, waits for them, and re-layouts, shards(): whole = lax.all_gather(s_blocks, 'cols', axis=2, tiled=True)  12.7 us
  transfers between devices with their start and end apart: 3, of which 3 were waited for; matrix products, arithmetic and copies ran while one was open for 5% of the time, Pallas kernels for 0%

commit v1 on v0

v1 whole, which is shorter than its diff:
```python
import functools

import jax
import jax.numpy as jnp
from jax import lax
from jax.experimental import pallas as pl
from jax.experimental.pallas import tpu as pltpu
from jax.sharding import PartitionSpec as P

MESH = pl.DeviceIdType.MESH
B = 64
PARTS = 4
KSP = 5
SPAN = 7
TILES = 20
CHUNKS = 6
QUADS = 16
VIEW = 5
ZERO_S = 160
X0, A0, C0, E0, D0, F0, G0 = 0, 4, 8, 10, 12, 16, 18


def place(row_count):
    r = lax.axis_index("rows")
    c = lax.axis_index("cols")
    x = c // 2
    outer = jnp.where(x == 0, (c == 0) & (r > 0), (c == 3) & (r < row_count - 1))
    skip = jnp.where(x == 0, jnp.where(outer, 0, 1), jnp.where(outer, 1, 0))
    first_quad = 8 * r - 4 * (1 - x) + 2 * skip
    return r, c, x, outer, skip, first_quad


def swap(v):
    return jnp.concatenate([v[:, B:], v[:, :B]], axis=1)


def kernel(
    row_count, s_ref, l_ref, t_ref, lt_ref, ct_ref, out_ref,
    near, table, dense_s, l_table, dense_l, total, send_sem, recv_sem,
):
    r, c, x, outer, skip, first_quad = place(row_count)
    k = c % 2
    up, down = r < row_count - 1, r > 0
    has_next = jnp.where(x == 0, up, down)
    has_prev = jnp.where(x == 0, down, up)
    next_row = jnp.where(x == 0, r + 1, r - 1)
    core = (r, 2 * x + 1 - k)
    across = (r, 2 * (1 - x) + k)
    ahead = (next_row, c)
    mine, theirs = c, 2 * (1 - x) + k
    low = lax.broadcasted_iota(jnp.int32, (B, 128), 1) < B

    def flip(t):
        return jnp.where(x == 1, t, 5 - t)

    def copy(src_chunk, dst_chunk, part, index, device):
        return pltpu.make_async_remote_copy(
            src_ref=near.at[src_chunk, part],
            dst_ref=near.at[dst_chunk, part],
            send_sem=send_sem.at[index],
            recv_sem=recv_sem.at[index],
            device_id=device,
            device_id_type=MESH,
        )

    def x_copy(s):
        return copy(jnp.where(x == 0, s + 2, 3 - s), jnp.where(x == 0, s, 5 - s), mine, X0 + s, across)

    def a_copy(s):
        return copy(flip(s), flip(s), mine, A0 + s, core)

    def c_copy(s):
        return copy(flip(s), flip(4 + s), mine, C0 + s, ahead)

    def e_copy(s):
        return copy(flip(s), flip(4 + s), theirs, E0 + s, ahead)

    def d_copy(s):
        return copy(flip(s), flip(s), theirs, D0 + s, core)

    def f_copy(s):
        return copy(flip(4 + s), flip(4 + s), mine, F0 + s, core)

    def g_copy(s):
        return copy(flip(4 + s), flip(4 + s), theirs, G0 + s, core)

    barrier = pltpu.get_barrier_semaphore()
    pl.semaphore_signal(barrier, inc=1, device_id=core, device_id_type=MESH)
    pl.semaphore_signal(barrier, inc=1, device_id=across, device_id_type=MESH)

    @pl.when(up)
    def _():
        pl.semaphore_signal(barrier, inc=1, device_id=(r + 1, c), device_id_type=MESH)

    @pl.when(down)
    def _():
        pl.semaphore_signal(barrier, inc=1, device_id=(r - 1, c), device_id_type=MESH)

    @pl.loop(0, 16)
    def _(pair):
        chunk = pair // 4 + 2 * (1 - x)
        at = lax.rem(pair, 4) * 5
        for odd in range(2):
            for t in range(2):
                near[chunk, mine, at + 2 * odd + t] = s_ref[2 * pair + odd, :, t * 128 : t * 128 + 128]
        near[chunk, mine, at + 4] = jnp.concatenate(
            [s_ref[2 * pair, :, 256:320], s_ref[2 * pair + 1, :, 256:320]], axis=1
        )

    pl.semaphore_wait(barrier, 2 + up.astype(jnp.int32) + down.astype(jnp.int32))

    for s in range(4):
        x_copy(s).start()
        if s < 2:

            @pl.when(has_next)
            def _():
                c_copy(s).start()

        a_copy(s).start()

    table[ZERO_S] = jnp.zeros((B, 128), jnp.bfloat16)
    l_table[30] = jnp.zeros((B, 128), jnp.bfloat16)

    @pl.loop(0, 8)
    def _(i):
        for t in range(15):
            v = l_ref[i, :, t * 128 : t * 128 + 128]
            l_table[t] = v
            l_table[15 + t] = swap(v)
        rows = pl.ds(pl.multiple_of(i * B, B), B)
        for quad in range(10):
            for half in range(2):
                at = quad * 4 + half * 2
                dense_l[quad, rows, half * 128 : half * 128 + 128] = jnp.where(
                    low, l_table[lt_ref[i, at]], l_table[lt_ref[i, at + 1]]
                )

    @pl.loop(0, 2 * QUADS + 1)
    def _(q):
        total[q] = jnp.zeros(total.shape[1:], jnp.float32)

    quad_count = 8 * row_count
    base_quad = jnp.clip(first_quad - 3, 0, quad_count - QUADS)

    def multiply(chunk):
        view = chunk - skip

        @pl.loop(0, PARTS)
        def _(p):
            for t in range(TILES):
                v = near[chunk, p, t]
                table[p * TILES + t] = v
                table[80 + p * TILES + t] = swap(v)

        @pl.loop(0, 2)
        def _(j):
            quad = view * 2 + j
            for row in range(4):
                for w in range(2 * SPAN):
                    dense_s[w // 2, row * B : row * B + B, (w % 2) * 128 : (w % 2) * 128 + 128] = jnp.where(
                        low,
                        table[t_ref[quad * 4 + row, 2 * w]],
                        table[t_ref[quad * 4 + row, 2 * w + 1]],
                    )
            start = 2 * (jnp.clip(first_quad + quad - 3, 0, quad_count - SPAN) - base_quad)
            for w in range(SPAN):
                part = jnp.dot(dense_l[quad], dense_s[w], preferred_element_type=jnp.float32)
                total[start + 2 * w] += part[:, :128]
                total[start + 2 * w + 1] += part[:, 128:]

    @pl.loop(0, 6)
    def _(e):
        for s, when in enumerate((0, 1, 3, 4)):

            @pl.when(e == when)
            def _():
                x_copy(s).wait_recv()
                d_copy(s).start()
                if s < 2:

                    @pl.when(has_next)
                    def _():
                        e_copy(s).start()

                a_copy(s).wait_recv()
                d_copy(s).wait_recv()

        for s, when in enumerate((2, 5)):

            @pl.when((e == when) & has_prev)
            def _():
                c_copy(s).wait_recv()
                f_copy(s).start()
                e_copy(s).wait_recv()
                g_copy(s).start()
                f_copy(s).wait_recv()
                g_copy(s).wait_recv()

        order = jnp.where(e < 2, e, jnp.where(e == 2, 4, jnp.where(e == 5, 5, e - 1)))

        @pl.when(jnp.where(outer, e >= 1, e <= 4))
        def _():
            multiply(flip(order))

    @pl.loop(0, 8)
    def _(i):
        rows = pl.ds(pl.multiple_of(i * B, B), B)
        for m in range(12):
            left, right = ct_ref[i, 2 * m], ct_ref[i, 2 * m + 1]
            a, b = total[left // 2, rows, :], total[right // 2, rows, :]
            a = jnp.where(left % 2 == 0, a, pltpu.roll(a, B, 1))
            b = jnp.where(right % 2 == 1, b, pltpu.roll(b, B, 1))
            out_ref[i, :, m * 128 : m * 128 + 128] = jnp.where(low, a, b).astype(jnp.bfloat16)

    for s in range(4):
        x_copy(s).wait_send()
        a_copy(s).wait_send()
        d_copy(s).wait_send()
    for s in range(2):

        @pl.when(has_next)
        def _():
            c_copy(s).wait_send()
            e_copy(s).wait_send()

        @pl.when(has_prev)
        def _():
            f_copy(s).wait_send()
            g_copy(s).wait_send()


def tables(row_count, l_index, s_cols, c_index):
    first_quad = place(row_count)[-1]
    quad_count = 8 * row_count
    rows = 4 * VIEW * 2
    row_ids = 4 * first_quad + lax.iota(jnp.int32, rows)
    near_cols = lax.dynamic_slice_in_dim(
        jnp.pad(s_cols, ((32, 32), (0, 0)), constant_values=-1), 4 * first_quad + 32, rows, axis=0
    )
    starts = 4 * jnp.clip(row_ids // 4 - 3, 0, quad_count - SPAN)
    at = lax.broadcasted_iota(jnp.int32, (rows, 4 * SPAN, PARTS * KSP), 0)
    col = lax.broadcasted_iota(jnp.int32, at.shape, 1)
    slot = lax.broadcasted_iota(jnp.int32, at.shape, 2)
    part, within = slot // KSP, slot % KSP
    odd = at % 2
    tile = jnp.where(within < 4, 2 * odd + within // 2, 4)
    half = jnp.where(within < 4, within % 2, odd)
    code = part * TILES + ((at // 2) % 4) * 5 + tile + 80 * (half != col % 2)
    hit = near_cols[:, None, :] == starts[:, None, None] + col
    s_table = ZERO_S + jnp.sum(jnp.where(hit, code - ZERO_S, 0), axis=2, dtype=jnp.int32)

    shape = (l_index.shape[0], rows, l_index.shape[1])
    at = lax.broadcasted_iota(jnp.int32, shape, 1)
    slot = lax.broadcasted_iota(jnp.int32, shape, 2)
    code = slot // 2 + 15 * (slot % 2 != at % 2)
    hit = l_index[:, None, :] == row_ids[None, :, None]
    l_table = 30 + jnp.sum(jnp.where(hit, code - 30, 0), axis=2, dtype=jnp.int32)

    spot = c_index - 4 * jnp.clip(first_quad - 3, 0, quad_count - QUADS)
    c_table = jnp.where((spot >= 0) & (spot < 4 * QUADS), spot, 4 * QUADS)
    return s_table, l_table, c_table


def shards(l_blocks, s_blocks, l_index, s_cols, c_index):
    row_count = lax.axis_size("rows")
    s_table, l_table, c_table = tables(row_count, l_index, s_cols, c_index)
    own = l_blocks.shape[0]
    vmem, smem = pl.BlockSpec(memory_space=pltpu.VMEM), pl.BlockSpec(memory_space=pltpu.SMEM)
    return pl.pallas_call(
        functools.partial(kernel, row_count),
        out_shape=jax.ShapeDtypeStruct((own, B, c_index.shape[1] * B), jnp.bfloat16),
        in_specs=[vmem, vmem, smem, smem, smem],
        out_specs=vmem,
        scratch_shapes=[
            pltpu.VMEM((CHUNKS, PARTS, TILES, B, 128), jnp.bfloat16),
            pltpu.VMEM((ZERO_S + 1, B, 128), jnp.bfloat16),
            pltpu.VMEM((SPAN, 4 * B, 4 * B), jnp.bfloat16),
            pltpu.VMEM((31, B, 128), jnp.bfloat16),
            pltpu.VMEM((2 * VIEW, own * B, 4 * B), jnp.bfloat16),
            pltpu.VMEM((2 * QUADS + 1, own * B, 128), jnp.float32),
            pltpu.SemaphoreType.DMA((20,)),
            pltpu.SemaphoreType.DMA((20,)),
        ],
        compiler_params=pltpu.CompilerParams(
            collective_id=0, has_side_effects=True, vmem_limit_bytes=56 * 1024 * 1024
        ),
        cost_estimate=pl.CostEstimate(flops=4_700_000_000, bytes_accessed=5_000_000, transcendentals=0),
    )(s_blocks, l_blocks, s_table, l_table, c_table)


def solution(mesh):
    return jax.shard_map(
        shards,
        mesh=mesh,
        in_specs=(
            P(("rows", "cols"), None, None),
            P("rows", None, "cols"),
            P(("rows", "cols"), None),
            P(),
            P(("rows", "cols"), None),
        ),
        out_specs=P(("rows", "cols"), None, None),
        check_vma=False,
    )
```

time: 419 us -> 54.3 us (0.13)
  the two profiles are of different devices: /device:TPU:19 before, /device:TPU:16 now
where the time goes in v1:
time: 54.3 us; the launch traced here: 54.1 us
  Pallas kernels  46.5 us (86%)
  local copies, waits for them, and re-layouts  4.32 us (8%)
  other arithmetic  3.14 us (6%)
    pallas_call x1, Pallas kernels, shards(): pl.pallas_call(functools.partial(kernel, row_count), out_shape=jax.ShapeD...  46.5 us
    unnamed x2, local copies, waits for them, and re-layouts  3.42 us
    select_n x1, other arithmetic, tables(): c_table = jnp.where((spot >= 0) & (spot < 4 * QUADS), spot, 4 * QUADS)  1.29 us

profile of v1, /device:TPU:16, one launch (start us, length us, event | category | flops | bytes accessed | tf_op | source)
XLA Modules:
  0.0 54.1 jit_solution(6827112601785271507)
XLA Ops:
  0.1 1.3 %and_select_fusion.ct_ref = s32[8,24]{1,0:T(8,128)} fusion(s32[8,24]{1,0:T(8,128)} %param.9, s32[]{:T(128)S(6)} %mul.59), kind=kLoop, calls=%fused_computation.36 | loop fusion | flops 960 | bytes 1540 | tf_op jit(solution)/shard_map/jit(_where)/select_n | solution.py:261
  1.4 0.8 %pad_dynamic-slice_fusion = s32[40,20]{0,1:T(8,128)S(1)} fusion(s32[]{:T(128)S(6)} %select_n.103, s32[256,20]{0,1:T(8,128)} %param.8), kind=kLoop, calls=%fused_computation.34 | loop fusion | bytes 23684 | tf_op jit(solution)/shard_map/dynamic_slice | solution.py:238
  2.2 0.3 fusion.5
  2.5 0.1 copy.9
  2.6 0.6 %broadcast_add_fusion.t_ref = s32[40,28]{1,0:T(8,128)} fusion(s32[40,28]{1,0:T(8,128)S(1)} %copy.9), kind=kLoop, calls=%fused_computation.35 | loop fusion | flops 1120 | bytes 8960 | tf_op jit(solution)/shard_map/add | solution.py:251
  3.2 0.8 %copy.11 = s32[8,30]{0,1:T(8,128)S(1)} copy(s32[8,30]{1,0:T(8,128)} %param.7) | data formatting | bytes 1920 | tf_op args[2]
  4.0 0.3 select_reduce_fusion
  4.3 0.6 %broadcast_add_fusion.1.lt_ref = s32[8,40]{1,0:T(8,128)} fusion(s32[8,40]{1,0:T(8,128)S(1)} %select_reduce_fusion), kind=kLoop, calls=%fused_computation.37 | loop fusion | flops 320 | bytes 2560 | tf_op jit(solution)/shard_map/add | solution.py:258
  4.9 46.5 %shard_map.55 = bf16[8,64,1536]{2,1,0:T(8,128)(2,1)} custom-call(bf16[32,64,320]{2,1,0:T(8,128)(2,1)} %s_ref.1, bf16[8,64,1920]{2,1,0:T(8,128)(2,1)} %l_ref.1, s32[40,28]{1,0:T(8,128)} %broadcast_add_fusion.t_ref, s32[8,40]{1,0:T(8,128)} %broadcast_add_fusion.1.lt_ref, s32[8,24]{1,0:T(8,128)} %and_select_fusion.ct_ref), custom_call_target="tpu_custom_call" | custom-call | flops 4700000256 | bytes 5000000 | tf_op jit(solution)/shard_map/pallas_call | solution.py:270
  51.4 2.7 %copy.13 = bf16[8,64,1536]{2,1,0:T(8,128)(2,1)} copy(bf16[8,64,1536]{2,1,0:T(8,128)(2,1)} %shard_map.55) | data formatting | bytes 3145728
  (12 shorter events, 0.1 us)

commit v2 on v1

v2 whole, which is shorter than its diff:
```python
import functools

import jax
import jax.numpy as jnp
from jax import lax
from jax.experimental import pallas as pl
from jax.experimental.pallas import tpu as pltpu
from jax.sharding import PartitionSpec as P

MESH = pl.DeviceIdType.MESH
B = 64
PARTS = 4
KSP = 5
SPAN = 8
TILES = 20
CHUNKS = 6
QUADS = 16
VIEW = 5
ZERO_S = 80
ZERO_L = 30
L_ROW, C_ROW = 40, 48
X0, A0, C0, E0, D0, F0, G0 = 0, 4, 8, 10, 12, 16, 18


def place(row_count):
    r = lax.axis_index("rows")
    c = lax.axis_index("cols")
    x = c // 2
    outer = jnp.where(x == 0, (c == 0) & (r > 0), (c == 3) & (r < row_count - 1))
    skip = jnp.where(x == 0, jnp.where(outer, 0, 1), jnp.where(outer, 1, 0))
    first_quad = 8 * r - 4 * (1 - x) + 2 * skip
    return r, c, x, outer, skip, first_quad


def swap(v):
    return jnp.concatenate([v[:, B:], v[:, :B]], axis=1)


def kernel(
    row_count, s_hbm, l_hbm, li_ref, sc_ref, ci_ref, out_hbm,
    s_ref, l_ref, out_ref, near, table, dense_s, l_table, dense_l, total, codes, spots,
    send_sem, recv_sem, in_sem, out_sem,
):
    r, c, x, outer, skip, first_quad = place(row_count)
    k = c % 2
    up, down = r < row_count - 1, r > 0
    has_next = jnp.where(x == 0, up, down)
    has_prev = jnp.where(x == 0, down, up)
    next_row = jnp.where(x == 0, r + 1, r - 1)
    core = (r, 2 * x + 1 - k)
    across = (r, 2 * (1 - x) + k)
    ahead = (next_row, c)
    mine, theirs = c, 2 * (1 - x) + k
    quad_count = 8 * row_count
    base_quad = jnp.clip(first_quad - 3, 0, quad_count - QUADS)

    barrier = pltpu.get_barrier_semaphore()
    pl.semaphore_signal(barrier, inc=1, device_id=core, device_id_type=MESH)
    pl.semaphore_signal(barrier, inc=1, device_id=across, device_id_type=MESH)

    @pl.when(up)
    def _():
        pl.semaphore_signal(barrier, inc=1, device_id=(r + 1, c), device_id_type=MESH)

    @pl.when(down)
    def _():
        pl.semaphore_signal(barrier, inc=1, device_id=(r - 1, c), device_id_type=MESH)

    s_in = pltpu.make_async_copy(s_hbm, s_ref, in_sem.at[0])
    l_in = pltpu.make_async_copy(l_hbm, l_ref, in_sem.at[1])
    s_in.start()
    l_in.start()

    low = lax.broadcasted_iota(jnp.int32, (B, 128), 1) < B

    def flip(t):
        return jnp.where(x == 1, t, 5 - t)

    def copy(src_chunk, dst_chunk, part, index, device):
        return pltpu.make_async_remote_copy(
            src_ref=near.at[src_chunk, part],
            dst_ref=near.at[dst_chunk, part],
            send_sem=send_sem.at[index],
            recv_sem=recv_sem.at[index],
            device_id=device,
            device_id_type=MESH,
        )

    def x_copy(s):
        return copy(jnp.where(x == 0, s + 2, 3 - s), jnp.where(x == 0, s, 5 - s), mine, X0 + s, across)

    def a_copy(s):
        return copy(flip(s), flip(s), mine, A0 + s, core)

    def c_copy(s):
        return copy(flip(s), flip(4 + s), mine, C0 + s, ahead)

    def e_copy(s):
        return copy(flip(s), flip(4 + s), theirs, E0 + s, ahead)

    def d_copy(s):
        return copy(flip(s), flip(s), theirs, D0 + s, core)

    def f_copy(s):
        return copy(flip(4 + s), flip(4 + s), mine, F0 + s, core)

    def g_copy(s):
        return copy(flip(4 + s), flip(4 + s), theirs, G0 + s, core)

    s_in.wait()

    @pl.loop(0, 16)
    def _(pair):
        chunk = pair // 4 + 2 * (1 - x)
        at = lax.rem(pair, 4) * 5
        for odd in range(2):
            for t in range(2):
                near[chunk, mine, at + 2 * odd + t] = s_ref[2 * pair + odd, :, t * 128 : t * 128 + 128]
        near[chunk, mine, at + 4] = jnp.concatenate(
            [s_ref[2 * pair, :, 256:320], s_ref[2 * pair + 1, :, 256:320]], axis=1
        )

    pl.semaphore_wait(barrier, 2 + up.astype(jnp.int32) + down.astype(jnp.int32))

    for s in range(4):
        x_copy(s).start()
        if s < 2:

            @pl.when(has_next)
            def _():
                c_copy(s).start()

        a_copy(s).start()

    row = lax.broadcasted_iota(jnp.int32, (8, 128), 0)
    lane = lax.broadcasted_iota(jnp.int32, (8, 128), 1)
    odd, side = row % 2, lane % 2
    for g in range(VIEW):
        first = 4 * first_quad + 8 * g
        inside = (first >= 0) & (first < 4 * quad_count)
        cols = sc_ref[pl.ds(pl.multiple_of(jnp.clip(first, 0, 4 * quad_count - 8), 8), 8), :]
        start = jnp.clip(first_quad + 2 * g - 3, 0, quad_count - SPAN)
        want = jnp.where(inside & (lane < 4 * SPAN), 4 * start + lane, -1)
        code = jnp.full((8, 128), ZERO_S, jnp.int32)
        for slot in range(PARTS * KSP):
            part, within = slot // KSP, slot % KSP
            tile = (part % 2) * TILES + (row // 2) * 5
            if within < 4:
                tile = tile + 2 * odd + within // 2 + jnp.where(side != within % 2, 40, 0)
            else:
                tile = tile + 4 + jnp.where(side != odd, 40, 0)
            code = jnp.where(cols[:, slot : slot + 1] == want, tile, code)
        codes[8 * g : 8 * g + 8, :] = code
    want = jnp.where(lane < 8 * VIEW, 4 * first_quad + lane, -1)
    code = jnp.full((8, 128), ZERO_L, jnp.int32)
    for slot in range(30):
        tile = slot // 2 + jnp.where(side != slot % 2, 15, 0)
        code = jnp.where(li_ref[:, slot : slot + 1] == want, tile, code)
    codes[L_ROW : L_ROW + 8, :] = code
    codes[C_ROW : C_ROW + 8, :] = jnp.zeros((8, 128), jnp.int32)
    spot = ci_ref[...] - 4 * base_quad
    codes[C_ROW : C_ROW + 8, 0 : spot.shape[1]] = jnp.where((spot >= 0) & (spot < 4 * QUADS), spot, 4 * QUADS)
    down_copy = pltpu.make_async_copy(codes, spots, in_sem.at[2])
    down_copy.start()

    @pl.loop(0, 2 * QUADS + 1)
    def _(q):
        total[q] = jnp.zeros(total.shape[1:], jnp.float32)

    table[ZERO_S] = jnp.zeros((B, 128), jnp.bfloat16)
    l_table[ZERO_L] = jnp.zeros((B, 128), jnp.bfloat16)
    down_copy.wait()
    l_in.wait()

    @pl.loop(0, 8)
    def _(i):
        for t in range(15):
            v = l_ref[i, :, t * 128 : t * 128 + 128]
            l_table[t] = v
            l_table[15 + t] = swap(v)
        rows = pl.ds(pl.multiple_of(i * B, B), B)
        for g in range(VIEW):
            for at in range(4):
                spot = 8 * g + 2 * at
                dense_l[g, rows, at * 128 : at * 128 + 128] = jnp.where(
                    low, l_table[spots[L_ROW + i, spot]], l_table[spots[L_ROW + i, spot + 1]]
                )

    def multiply(chunk, half):
        view = chunk - skip

        @pl.loop(0, 2)
        def _(p):
            for t in range(TILES):
                v = near[chunk, 2 * half + p, t]
                table[p * TILES + t] = v
                table[40 + p * TILES + t] = swap(v)

        start = jnp.clip(first_quad + 2 * view - 3, 0, quad_count - SPAN) - base_quad

        @pl.loop(0, 4)
        def _(n):
            for row in range(8):
                for w in range(2):
                    spot = 8 * n + 4 * w + 2 * half
                    dense_s[n, row * B : row * B + B, w * 128 : w * 128 + 128] = jnp.where(
                        low, table[spots[view * 8 + row, spot]], table[spots[view * 8 + row, spot + 1]]
                    )
            part = jnp.dot(dense_l[view], dense_s[n], preferred_element_type=jnp.float32)
            at = 2 * (start + 2 * n) + half
            total[at] += part[:, :128]
            total[at + 2] += part[:, 128:]

    events = ("A0", "A1", "A2", "A3", "X0", "C0", "X1", "C1", "E0", "X2", "X3", "E1")

    @pl.loop(0, len(events))
    def _(e):
        order = e * 0
        for index, (kind, s) in enumerate(events):
            s = int(s)
            order = jnp.where(e == index, s if kind in "AX" else 4 + s, order)

            @pl.when((e == index) & (has_prev if kind in "CE" else e >= 0))
            def _():
                if kind == "A":
                    a_copy(s).wait_recv()
                elif kind == "X":
                    x_copy(s).wait_recv()
                    d_copy(s).start()
                    if s < 2:

                        @pl.when(has_next)
                        def _():
                            e_copy(s).start()

                    d_copy(s).wait_recv()
                elif kind == "C":
                    c_copy(s).wait_recv()
                    f_copy(s).start()
                    f_copy(s).wait_recv()
                else:
                    e_copy(s).wait_recv()
                    g_copy(s).start()
                    g_copy(s).wait_recv()

        own_half = e * 0
        for index, (kind, s) in enumerate(events):
            own_half = jnp.where(e == index, 1 if kind in "AC" else 0, own_half)
        halo = order >= 4

        @pl.when(jnp.where(outer, order != 0, order != 5) & (has_prev | jnp.logical_not(halo)))
        def _():
            multiply(flip(order), jnp.where(own_half == 1, x, 1 - x))

    @pl.loop(0, 8)
    def _(i):
        rows = pl.ds(pl.multiple_of(i * B, B), B)
        for m in range(12):
            left, right = spots[C_ROW + i, 2 * m], spots[C_ROW + i, 2 * m + 1]
            a, b = total[left // 2, rows, :], total[right // 2, rows, :]
            straight = jnp.where(low, a, b)
            crossed = pltpu.roll(jnp.where(low, b, a), B, 1)
            keep = jnp.where(low, 1 - left % 2, right % 2) == 1
            out_ref[i, :, m * 128 : m * 128 + 128] = jnp.where(keep, straight, crossed).astype(jnp.bfloat16)
        pltpu.make_async_copy(out_ref.at[i], out_hbm.at[i], out_sem.at[i]).start()

    for s in range(4):
        x_copy(s).wait_send()
        a_copy(s).wait_send()
        d_copy(s).wait_send()
    for s in range(2):

        @pl.when(has_next)
        def _():
            c_copy(s).wait_send()
            e_copy(s).wait_send()

        @pl.when(has_prev)
        def _():
            f_copy(s).wait_send()
            g_copy(s).wait_send()

    @pl.loop(0, 8)
    def _(i):
        pltpu.make_async_copy(out_ref.at[i], out_hbm.at[i], out_sem.at[i]).wait()


def shards(l_blocks, s_blocks, l_index, s_cols, c_index):
    row_count = lax.axis_size("rows")
    own, kept = l_blocks.shape[0], c_index.shape[1]
    vmem, hbm = pl.BlockSpec(memory_space=pltpu.VMEM), pl.BlockSpec(memory_space=pl.ANY)
    return pl.pallas_call(
        functools.partial(kernel, row_count),
        out_shape=jax.ShapeDtypeStruct((own, B, kept * B), jnp.bfloat16),
        in_specs=[hbm, hbm, vmem, vmem, vmem],
        out_specs=hbm,
        scratch_shapes=[
            pltpu.VMEM(s_blocks.shape, jnp.bfloat16),
            pltpu.VMEM(l_blocks.shape, jnp.bfloat16),
            pltpu.VMEM((own, B, kept * B), jnp.bfloat16),
            pltpu.VMEM((CHUNKS, PARTS, TILES, B, 128), jnp.bfloat16),
            pltpu.VMEM((ZERO_S + 1, B, 128), jnp.bfloat16),
            pltpu.VMEM((4, 8 * B, 4 * B), jnp.bfloat16),
            pltpu.VMEM((ZERO_L + 1, B, 128), jnp.bfloat16),
            pltpu.VMEM((VIEW, own * B, 8 * B), jnp.bfloat16),
            pltpu.VMEM((2 * QUADS + 1, own * B, 128), jnp.float32),
            pltpu.VMEM((C_ROW + 8, 128), jnp.int32),
            pltpu.SMEM((C_ROW + 8, 128), jnp.int32),
            pltpu.SemaphoreType.DMA((20,)),
            pltpu.SemaphoreType.DMA((20,)),
            pltpu.SemaphoreType.DMA((3,)),
            pltpu.SemaphoreType.DMA((8,)),
        ],
        compiler_params=pltpu.CompilerParams(
            collective_id=0, has_side_effects=True, vmem_limit_bytes=56 * 1024 * 1024
        ),
        cost_estimate=pl.CostEstimate(flops=4_700_000_000, bytes_accessed=5_000_000, transcendentals=0),
    )(s_blocks, l_blocks, l_index, s_cols, c_index)


def solution(mesh):
    return jax.shard_map(
        shards,
        mesh=mesh,
        in_specs=(
            P(("rows", "cols"), None, None),
            P("rows", None, "cols"),
            P(("rows", "cols"), None),
            P(),
            P(("rows", "cols"), None),
        ),
        out_specs=P(("rows", "cols"), None, None),
        check_vma=False,
    )
```

time: 54.3 us -> 47.9 us (0.88)
  the two profiles are of different devices: /device:TPU:16 before, /device:TPU:19 now
where the time goes in v2:
time: 47.9 us; the launch traced here: 46.9 us
  Pallas kernels  42.8 us (89%)
  local copies, waits for them, and re-layouts  4.15 us (9%)
    pallas_call x1, Pallas kernels, shards(): pl.pallas_call(functools.partial(kernel, row_count), out_shape=jax.ShapeD...  42.8 us
    unnamed x2, local copies, waits for them, and re-layouts  4.15 us

profile of v2, /device:TPU:19, one launch (start us, length us, event | category | flops | bytes accessed | tf_op | source)
XLA Modules:
  0.0 46.9 jit_solution(6384392323268937809)
XLA Ops:
  0.0 1.5 %copy.6.sc_ref = s32[256,20]{1,0:T(8,128)} copy(s32[256,20]{0,1:T(8,128)} %param.8) | data formatting | bytes 40960 | tf_op args[3]
  1.5 42.8 %shard_map.55 = bf16[8,64,1536]{2,1,0:T(8,128)(2,1)} custom-call(bf16[32,64,320]{2,1,0:T(8,128)(2,1)} %s_hbm.1, bf16[8,64,1920]{2,1,0:T(8,128)(2,1)} %l_hbm.1, s32[8,30]{1,0:T(8,128)} %li_ref.1, s32[256,20]{1,0:T(8,128)} %copy.6.sc_ref, s32[8,24]{1,0:T(8,128)} %ci_ref.1), custom_call_target="tpu_custom_call" | custom-call | flops 4700000256 | bytes 5000000 | tf_op jit(solution)/shard_map/pallas_call | solution.py:292
  44.3 2.7 %copy.8 = bf16[8,64,1536]{2,1,0:T(8,128)(2,1)} copy(bf16[8,64,1536]{2,1,0:T(8,128)(2,1)} %shard_map.55) | data formatting | bytes 3145728

commit v3 on v2

--- a/solution.py
+++ b/solution.py
@@ -18,7 +18,7 @@
 VIEW = 5
 ZERO_S = 80
 ZERO_L = 30
-L_ROW, C_ROW = 40, 48
+L_ROW, C_ROW = 32, 40
 X0, A0, C0, E0, D0, F0, G0 = 0, 4, 8, 10, 12, 16, 18
 
 
@@ -37,9 +37,9 @@
 
 
 def kernel(
-    row_count, s_hbm, l_hbm, li_ref, sc_ref, ci_ref, out_hbm,
-    s_ref, l_ref, out_ref, near, table, dense_s, l_table, dense_l, total, codes, spots,
-    send_sem, recv_sem, in_sem, out_sem,
+    row_count, s_hbm, l_hbm, li_ref, sc_ref, ci_ref, out_ref,
+    s_ref, l_ref, near, table, dense_s, l_table, dense_l, total, codes, spots,
+    send_sem, recv_sem, in_sem,
 ):
     r, c, x, outer, skip, first_quad = place(row_count)
     k = c % 2
@@ -132,32 +132,32 @@
 
         a_copy(s).start()
 
-    row = lax.broadcasted_iota(jnp.int32, (8, 128), 0)
-    lane = lax.broadcasted_iota(jnp.int32, (8, 128), 1)
-    odd, side = row % 2, lane % 2
-    for g in range(VIEW):
-        first = 4 * first_quad + 8 * g
-        inside = (first >= 0) & (first < 4 * quad_count)
-        cols = sc_ref[pl.ds(pl.multiple_of(jnp.clip(first, 0, 4 * quad_count - 8), 8), 8), :]
-        start = jnp.clip(first_quad + 2 * g - 3, 0, quad_count - SPAN)
-        want = jnp.where(inside & (lane < 4 * SPAN), 4 * start + lane, -1)
-        code = jnp.full((8, 128), ZERO_S, jnp.int32)
-        for slot in range(PARTS * KSP):
-            part, within = slot // KSP, slot % KSP
-            tile = (part % 2) * TILES + (row // 2) * 5
-            if within < 4:
-                tile = tile + 2 * odd + within // 2 + jnp.where(side != within % 2, 40, 0)
-            else:
-                tile = tile + 4 + jnp.where(side != odd, 40, 0)
-            code = jnp.where(cols[:, slot : slot + 1] == want, tile, code)
-        codes[8 * g : 8 * g + 8, :] = code
+    base_row = 128 * jnp.clip(4 * first_quad // 128, 0, 4 * quad_count // 128 - 2)
+    cols = sc_ref[:, pl.ds(pl.multiple_of(base_row, 128), 256)]
+    want_at = lax.broadcasted_iota(jnp.int32, (4 * SPAN, 256), 0)
+    row = lax.broadcasted_iota(jnp.int32, (4 * SPAN, 256), 1)
+    odd, side = row % 2, want_at % 2
+    want = 4 * jnp.clip(2 * ((base_row + row) // 8) - 3, 0, quad_count - SPAN) + want_at
+    first_tile = ((row // 2) % 4) * 5
+    code = jnp.full((4 * SPAN, 256), ZERO_S, jnp.int32)
+    for within in range(KSP):
+        if within < 4:
+            tile = first_tile + 2 * odd + within // 2 + jnp.where(side != within % 2, 40, 0)
+        else:
+            tile = first_tile + 4 + jnp.where(side != odd, 40, 0)
+        for part in range(PARTS):
+            slot = part * KSP + within
+            code = jnp.where(cols[slot : slot + 1, :] == want, tile + (part % 2) * TILES, code)
+    codes[0 : 4 * SPAN, :] = code
+    lane = lax.broadcasted_iota(jnp.int32, (8, 256), 1)
+    side = lane % 2
     want = jnp.where(lane < 8 * VIEW, 4 * first_quad + lane, -1)
-    code = jnp.full((8, 128), ZERO_L, jnp.int32)
+    code = jnp.full((8, 256), ZERO_L, jnp.int32)
     for slot in range(30):
         tile = slot // 2 + jnp.where(side != slot % 2, 15, 0)
         code = jnp.where(li_ref[:, slot : slot + 1] == want, tile, code)
     codes[L_ROW : L_ROW + 8, :] = code
-    codes[C_ROW : C_ROW + 8, :] = jnp.zeros((8, 128), jnp.int32)
+    codes[C_ROW : C_ROW + 8, :] = jnp.zeros((8, 256), jnp.int32)
     spot = ci_ref[...] - 4 * base_quad
     codes[C_ROW : C_ROW + 8, 0 : spot.shape[1]] = jnp.where((spot >= 0) & (spot < 4 * QUADS), spot, 4 * QUADS)
     down_copy = pltpu.make_async_copy(codes, spots, in_sem.at[2])
@@ -197,6 +197,7 @@
                 table[40 + p * TILES + t] = swap(v)
 
         start = jnp.clip(first_quad + 2 * view - 3, 0, quad_count - SPAN) - base_quad
+        first = 4 * first_quad - base_row + view * 8
 
         @pl.loop(0, 4)
         def _(n):
@@ -204,7 +205,7 @@
                 for w in range(2):
                     spot = 8 * n + 4 * w + 2 * half
                     dense_s[n, row * B : row * B + B, w * 128 : w * 128 + 128] = jnp.where(
-                        low, table[spots[view * 8 + row, spot]], table[spots[view * 8 + row, spot + 1]]
+                        low, table[spots[spot, first + row]], table[spots[spot + 1, first + row]]
                     )
             part = jnp.dot(dense_l[view], dense_s[n], preferred_element_type=jnp.float32)
             at = 2 * (start + 2 * n) + half
@@ -262,7 +263,6 @@
             crossed = pltpu.roll(jnp.where(low, b, a), B, 1)
             keep = jnp.where(low, 1 - left % 2, right % 2) == 1
             out_ref[i, :, m * 128 : m * 128 + 128] = jnp.where(keep, straight, crossed).astype(jnp.bfloat16)
-        pltpu.make_async_copy(out_ref.at[i], out_hbm.at[i], out_sem.at[i]).start()
 
     for s in range(4):
         x_copy(s).wait_send()
@@ -279,10 +279,6 @@
         def _():
             f_copy(s).wait_send()
             g_copy(s).wait_send()
-
-    @pl.loop(0, 8)
-    def _(i):
-        pltpu.make_async_copy(out_ref.at[i], out_hbm.at[i], out_sem.at[i]).wait()
 
 
 def shards(l_blocks, s_blocks, l_index, s_cols, c_index):
@@ -291,31 +287,29 @@
     vmem, hbm = pl.BlockSpec(memory_space=pltpu.VMEM), pl.BlockSpec(memory_space=pl.ANY)
     return pl.pallas_call(
         functools.partial(kernel, row_count),
-        out_shape=jax.ShapeDtypeStruct((own, B, kept * B), jnp.bfloat16),
+        out_shape=pltpu.VMEM((own, B, kept * B), jnp.bfloat16),
         in_specs=[hbm, hbm, vmem, vmem, vmem],
-        out_specs=hbm,
+        out_specs=vmem,
         scratch_shapes=[
             pltpu.VMEM(s_blocks.shape, jnp.bfloat16),
             pltpu.VMEM(l_blocks.shape, jnp.bfloat16),
-            pltpu.VMEM((own, B, kept * B), jnp.bfloat16),
             pltpu.VMEM((CHUNKS, PARTS, TILES, B, 128), jnp.bfloat16),
             pltpu.VMEM((ZERO_S + 1, B, 128), jnp.bfloat16),
             pltpu.VMEM((4, 8 * B, 4 * B), jnp.bfloat16),
             pltpu.VMEM((ZERO_L + 1, B, 128), jnp.bfloat16),
             pltpu.VMEM((VIEW, own * B, 8 * B), jnp.bfloat16),
             pltpu.VMEM((2 * QUADS + 1, own * B, 128), jnp.float32),
-            pltpu.VMEM((C_ROW + 8, 128), jnp.int32),
-            pltpu.SMEM((C_ROW + 8, 128), jnp.int32),
+            pltpu.VMEM((C_ROW + 8, 256), jnp.int32),
+            pltpu.SMEM((C_ROW + 8, 256), jnp.int32),
             pltpu.SemaphoreType.DMA((20,)),
             pltpu.SemaphoreType.DMA((20,)),
             pltpu.SemaphoreType.DMA((3,)),
-            pltpu.SemaphoreType.DMA((8,)),
         ],
         compiler_params=pltpu.CompilerParams(
             collective_id=0, has_side_effects=True, vmem_limit_bytes=56 * 1024 * 1024
         ),
         cost_estimate=pl.CostEstimate(flops=4_700_000_000, bytes_accessed=5_000_000, transcendentals=0),
-    )(s_blocks, l_blocks, l_index, s_cols, c_index)
+    )(s_blocks, l_blocks, l_index, s_cols.T, c_index)
 
 
 def solution(mesh):

time: 47.9 us -> 44.1 us (0.921)
  local copies, waits for them, and re-layouts: 4.15 us -> 1.15 us
    unnamed x2 -> x1, local copies, waits for them, and re-layouts: 4.15 us -> 1.15 us
where the time goes in v3:
time: 44.1 us; the launch traced here: 43.6 us
  Pallas kernels  42.4 us (96%)
  local copies, waits for them, and re-layouts  1.15 us (3%)
    pallas_call x1, Pallas kernels, shards(): pl.pallas_call(functools.partial(kernel, row_count), out_shape=pltpu.VMEM...  42.4 us
    unnamed x1, local copies, waits for them, and re-layouts  1.15 us

profile of v3, /device:TPU:19, one launch (start us, length us, event | category | flops | bytes accessed | tf_op | source)
XLA Modules:
  0.0 43.6 jit_solution(12418055621365522487)
XLA Ops:
  0.0 42.4 %shard_map.55 = bf16[8,64,1536]{2,1,0:T(8,128)(2,1)S(1)} custom-call(bf16[32,64,320]{2,1,0:T(8,128)(2,1)} %s_hbm.1, bf16[8,64,1920]{2,1,0:T(8,128)(2,1)} %l_hbm.1, s32[8,30]{1,0:T(8,128)} %li_ref.1, s32[20,256]{1,0:T(8,128)} %bitcast.1, s32[8,24]{1,0:T(8,128)} %ci_ref.1), custom_call_target="tpu_custom_call" | custom-call | flops 4700000256 | bytes 5000000 | tf_op jit(solution)/shard_map/pallas_call | solution.py:288
  42.4 1.1 %copy.7 = bf16[8,64,1536]{2,1,0:T(8,128)(2,1)} copy(bf16[8,64,1536]{2,1,0:T(8,128)(2,1)S(1)} %shard_map.55) | data formatting | bytes 3145728

commit v4 on v3

--- a/solution.py
+++ b/solution.py
@@ -109,28 +109,32 @@
 
     s_in.wait()
 
-    @pl.loop(0, 16)
-    def _(pair):
-        chunk = pair // 4 + 2 * (1 - x)
-        at = lax.rem(pair, 4) * 5
-        for odd in range(2):
-            for t in range(2):
-                near[chunk, mine, at + 2 * odd + t] = s_ref[2 * pair + odd, :, t * 128 : t * 128 + 128]
-        near[chunk, mine, at + 4] = jnp.concatenate(
-            [s_ref[2 * pair, :, 256:320], s_ref[2 * pair + 1, :, 256:320]], axis=1
-        )
-
-    pl.semaphore_wait(barrier, 2 + up.astype(jnp.int32) + down.astype(jnp.int32))
-
-    for s in range(4):
-        x_copy(s).start()
-        if s < 2:
+    for step in (0, 3, 1, 2):
+        group_chunk = jnp.where(x == 0, step, 3 - step)
+        chunk = group_chunk + 2 * (1 - x)
+
+        @pl.loop(0, 4)
+        def _(pair):
+            at = pair * 5
+            source = 8 * group_chunk + 2 * pair
+            for odd in range(2):
+                for t in range(2):
+                    near[chunk, mine, at + 2 * odd + t] = s_ref[source + odd, :, t * 128 : t * 128 + 128]
+            near[chunk, mine, at + 4] = jnp.concatenate(
+                [s_ref[source, :, 256:320], s_ref[source + 1, :, 256:320]], axis=1
+            )
+
+        if step == 0:
+            pl.semaphore_wait(barrier, 2 + up.astype(jnp.int32) + down.astype(jnp.int32))
+        if step < 2:
+            x_copy(step).start()
+        else:
 
             @pl.when(has_next)
             def _():
-                c_copy(s).start()
-
-        a_copy(s).start()
+                c_copy(3 - step).start()
+
+        a_copy(3 - step).start()
 
     base_row = 128 * jnp.clip(4 * first_quad // 128, 0, 4 * quad_count // 128 - 2)
     cols = sc_ref[:, pl.ds(pl.multiple_of(base_row, 128), 256)]
@@ -227,13 +231,14 @@
                     a_copy(s).wait_recv()
                 elif kind == "X":
                     x_copy(s).wait_recv()
-                    d_copy(s).start()
                     if s < 2:
 
                         @pl.when(has_next)
                         def _():
                             e_copy(s).start()
 
+                        x_copy(s + 2).start()
+                    d_copy(s).start()
                     d_copy(s).wait_recv()
                 elif kind == "C":
                     c_copy(s).wait_recv()

time: 44.1 us -> 43.8 us (level)
  no operation moved by 1% of the time
where the time goes in v4:
time: 43.8 us; the launch traced here: 43.7 us
  Pallas kernels  42.5 us (97%)
  local copies, waits for them, and re-layouts  1.15 us (3%)
    pallas_call x1, Pallas kernels, shards(): pl.pallas_call(functools.partial(kernel, row_count), out_shape=pltpu.VMEM...  42.5 us
    unnamed x1, local copies, waits for them, and re-layouts  1.15 us

profile of v4, /device:TPU:19, one launch (start us, length us, event | category | flops | bytes accessed | tf_op | source)
XLA Modules:
  0.0 43.7 jit_solution(11867947370434035698)
XLA Ops:
  0.0 42.5 %shard_map.55 = bf16[8,64,1536]{2,1,0:T(8,128)(2,1)S(1)} custom-call(bf16[32,64,320]{2,1,0:T(8,128)(2,1)} %s_hbm.1, bf16[8,64,1920]{2,1,0:T(8,128)(2,1)} %l_hbm.1, s32[8,30]{1,0:T(8,128)} %li_ref.1, s32[20,256]{1,0:T(8,128)} %bitcast.1, s32[8,24]{1,0:T(8,128)} %ci_ref.1), custom_call_target="tpu_custom_call" | custom-call | flops 4700000256 | bytes 5000000 | tf_op jit(solution)/shard_map/pallas_call | solution.py:293
  42.5 1.1 %copy.7 = bf16[8,64,1536]{2,1,0:T(8,128)(2,1)} copy(bf16[8,64,1536]{2,1,0:T(8,128)(2,1)S(1)} %shard_map.55) | data formatting | bytes 3145728

commit v5 on v4

--- a/solution.py
+++ b/solution.py
@@ -72,6 +72,7 @@
     l_in.start()
 
     low = lax.broadcasted_iota(jnp.int32, (B, 128), 1) < B
+    low16 = lax.broadcasted_iota(jnp.int16, (B, 128), 1) < B
 
     def flip(t):
         return jnp.where(x == 1, t, 5 - t)
@@ -187,7 +188,7 @@
             for at in range(4):
                 spot = 8 * g + 2 * at
                 dense_l[g, rows, at * 128 : at * 128 + 128] = jnp.where(
-                    low, l_table[spots[L_ROW + i, spot]], l_table[spots[L_ROW + i, spot + 1]]
+                    low16, l_table[spots[L_ROW + i, spot]], l_table[spots[L_ROW + i, spot + 1]]
                 )
 
     def multiply(chunk, half):
@@ -203,51 +204,60 @@
         start = jnp.clip(first_quad + 2 * view - 3, 0, quad_count - SPAN) - base_quad
         first = 4 * first_quad - base_row + view * 8
 
-        @pl.loop(0, 4)
-        def _(n):
+        for n in range(4):
             for row in range(8):
                 for w in range(2):
                     spot = 8 * n + 4 * w + 2 * half
                     dense_s[n, row * B : row * B + B, w * 128 : w * 128 + 128] = jnp.where(
-                        low, table[spots[spot, first + row]], table[spots[spot + 1, first + row]]
+                        low16, table[spots[spot, first + row]], table[spots[spot + 1, first + row]]
                     )
             part = jnp.dot(dense_l[view], dense_s[n], preferred_element_type=jnp.float32)
             at = 2 * (start + 2 * n) + half
             total[at] += part[:, :128]
             total[at + 2] += part[:, 128:]
 
-    events = ("A0", "A1", "A2", "A3", "X0", "C0", "X1", "C1", "E0", "X2", "X3", "E1")
+    events = ("A0", "A1", "X0", "C0", "A2", "X1", "C1", "A3", "E0", "X2", "X3", "E1")
+
+    def when_prev(action):
+        pl.when(has_prev)(action)
+
+    def arrive_x(s):
+        x_copy(s).wait_recv()
+        if s < 2:
+            pl.when(has_next)(lambda: e_copy(s).start())
+            x_copy(s + 2).start()
+        d_copy(s).start()
+
+    def arrive_c(s):
+        c_copy(s).wait_recv()
+        f_copy(s).start()
+
+    def arrive_e(s):
+        e_copy(s).wait_recv()
+        g_copy(s).start()
+
+    def before(kind, s):
+        if kind == "A":
+            a_copy(s).wait_recv()
+        elif kind == "X":
+            if s != 2:
+                arrive_x(s)
+                when_prev(lambda: arrive_e(1) if s == 3 else arrive_c(s))
+            d_copy(s).wait_recv()
+        elif kind == "C":
+            when_prev(lambda: f_copy(s).wait_recv())
+        else:
+            if s == 0:
+                when_prev(lambda: arrive_e(0))
+                arrive_x(2)
+            when_prev(lambda: g_copy(s).wait_recv())
 
     @pl.loop(0, len(events))
     def _(e):
         order = e * 0
         for index, (kind, s) in enumerate(events):
-            s = int(s)
-            order = jnp.where(e == index, s if kind in "AX" else 4 + s, order)
-
-            @pl.when((e == index) & (has_prev if kind in "CE" else e >= 0))
-            def _():
-                if kind == "A":
-                    a_copy(s).wait_recv()
-                elif kind == "X":
-                    x_copy(s).wait_recv()
-                    if s < 2:
-
-                        @pl.when(has_next)
-                        def _():
-                            e_copy(s).start()
-
-                        x_copy(s + 2).start()
-                    d_copy(s).start()
-                    d_copy(s).wait_recv()
-                elif kind == "C":
-                    c_copy(s).wait_recv()
-                    f_copy(s).start()
-                    f_copy(s).wait_recv()
-                else:
-                    e_copy(s).wait_recv()
-                    g_copy(s).start()
-                    g_copy(s).wait_recv()
+            order = jnp.where(e == index, int(s) if kind in "AX" else 4 + int(s), order)
+            pl.when(e == index)(functools.partial(before, kind, int(s)))
 
         own_half = e * 0
         for index, (kind, s) in enumerate(events):

time: 43.8 us -> 40.1 us (0.916); the launches traced: 43.7 us -> 39.4 us
  Pallas kernels: 42.5 us -> 38.3 us
    pallas_call x1, Pallas kernels: 42.5 us -> 38.3 us  [shards(): pl.pallas_call(functools.partial(kernel, row_count), out_shape=pltpu.VMEM...]
where the time goes in v5:
time: 40.1 us; the launch traced here: 39.4 us
  Pallas kernels  38.3 us (96%)
  local copies, waits for them, and re-layouts  1.15 us (3%)
    pallas_call x1, Pallas kernels, shards(): pl.pallas_call(functools.partial(kernel, row_count), out_shape=pltpu.VMEM...  38.3 us
    unnamed x1, local copies, waits for them, and re-layouts  1.15 us

profile of v5, /device:TPU:19, one launch (start us, length us, event | category | flops | bytes accessed | tf_op | source)
XLA Modules:
  0.0 39.4 jit_solution(9688303429964306280)
XLA Ops:
  0.0 38.3 %shard_map.55 = bf16[8,64,1536]{2,1,0:T(8,128)(2,1)S(1)} custom-call(bf16[32,64,320]{2,1,0:T(8,128)(2,1)} %s_hbm.1, bf16[8,64,1920]{2,1,0:T(8,128)(2,1)} %l_hbm.1, s32[8,30]{1,0:T(8,128)} %li_ref.1, s32[20,256]{1,0:T(8,128)} %bitcast.1, s32[8,24]{1,0:T(8,128)} %ci_ref.1), custom_call_target="tpu_custom_call" | custom-call | flops 4700000256 | bytes 5000000 | tf_op jit(solution)/shard_map/pallas_call | solution.py:303
  38.3 1.1 %copy.7 = bf16[8,64,1536]{2,1,0:T(8,128)(2,1)} copy(bf16[8,64,1536]{2,1,0:T(8,128)(2,1)S(1)} %shard_map.55) | data formatting | bytes 3145728

commit v6 on v5

--- a/solution.py
+++ b/solution.py
@@ -20,6 +20,8 @@
 ZERO_L = 30
 L_ROW, C_ROW = 32, 40
 X0, A0, C0, E0, D0, F0, G0 = 0, 4, 8, 10, 12, 16, 18
+LATE = 20
+PIECE = TILES // 2
 
 
 def place(row_count):
@@ -37,8 +39,8 @@
 
 
 def kernel(
-    row_count, s_hbm, l_hbm, li_ref, sc_ref, ci_ref, out_ref,
-    s_ref, l_ref, near, table, dense_s, l_table, dense_l, total, codes, spots,
+    row_count, s_hbm, l_hbm, li_hbm, sc_hbm, ci_hbm, out_ref,
+    s_ref, l_ref, li_ref, sc_ref, ci_ref, near, table, dense_s, l_table, dense_l, total, codes, spots,
     send_sem, recv_sem, in_sem,
 ):
     r, c, x, outer, skip, first_quad = place(row_count)
@@ -66,9 +68,19 @@
     def _():
         pl.semaphore_signal(barrier, inc=1, device_id=(r - 1, c), device_id_type=MESH)
 
-    s_in = pltpu.make_async_copy(s_hbm, s_ref, in_sem.at[0])
-    l_in = pltpu.make_async_copy(l_hbm, l_ref, in_sem.at[1])
-    s_in.start()
+    def s_in(step):
+        rows = pl.ds(8 * jnp.where(x == 0, step, 3 - step), 8)
+        return pltpu.make_async_copy(s_hbm.at[rows], s_ref.at[rows], in_sem.at[step])
+
+    for step in (0, 3, 1, 2):
+        s_in(step).start()
+    small_in = [
+        pltpu.make_async_copy(source, target, in_sem.at[4 + n])
+        for n, (source, target) in enumerate(((sc_hbm, sc_ref), (li_hbm, li_ref), (ci_hbm, ci_ref), (l_hbm, l_ref)))
+    ]
+    l_in = small_in.pop()
+    for operand in small_in:
+        operand.start()
     l_in.start()
 
     low = lax.broadcasted_iota(jnp.int32, (B, 128), 1) < B
@@ -77,18 +89,21 @@
     def flip(t):
         return jnp.where(x == 1, t, 5 - t)
 
-    def copy(src_chunk, dst_chunk, part, index, device):
+    def copy(src_chunk, dst_chunk, part, index, device, piece=None):
+        tiles = slice(None) if piece is None else pl.ds(piece * PIECE, PIECE)
+        index = index if not piece else LATE + (index - X0) // 4
         return pltpu.make_async_remote_copy(
-            src_ref=near.at[src_chunk, part],
-            dst_ref=near.at[dst_chunk, part],
+            src_ref=near.at[src_chunk, part, tiles],
+            dst_ref=near.at[dst_chunk, part, tiles],
             send_sem=send_sem.at[index],
             recv_sem=recv_sem.at[index],
             device_id=device,
             device_id_type=MESH,
         )
 
-    def x_copy(s):
-        return copy(jnp.where(x == 0, s + 2, 3 - s), jnp.where(x == 0, s, 5 - s), mine, X0 + s, across)
+    def x_copy(s, piece=None):
+        source, target = jnp.where(x == 0, s + 2, 3 - s), jnp.where(x == 0, s, 5 - s)
+        return copy(source, target, mine, X0 + s, across, piece)
 
     def a_copy(s):
         return copy(flip(s), flip(s), mine, A0 + s, core)
@@ -96,23 +111,25 @@
     def c_copy(s):
         return copy(flip(s), flip(4 + s), mine, C0 + s, ahead)
 
-    def e_copy(s):
-        return copy(flip(s), flip(4 + s), theirs, E0 + s, ahead)
-
-    def d_copy(s):
-        return copy(flip(s), flip(s), theirs, D0 + s, core)
+    def e_copy(s, piece=None):
+        return copy(flip(s), flip(4 + s), theirs, E0 + s, ahead, piece)
+
+    def d_copy(s, piece=None):
+        return copy(flip(s), flip(s), theirs, D0 + s, core, piece)
 
     def f_copy(s):
         return copy(flip(4 + s), flip(4 + s), mine, F0 + s, core)
 
-    def g_copy(s):
-        return copy(flip(4 + s), flip(4 + s), theirs, G0 + s, core)
-
-    s_in.wait()
+    def g_copy(s, piece=None):
+        return copy(flip(4 + s), flip(4 + s), theirs, G0 + s, core, piece)
+
+    def pieces(s, last):
+        return (0, 1) if s == last else (None,)
 
     for step in (0, 3, 1, 2):
         group_chunk = jnp.where(x == 0, step, 3 - step)
         chunk = group_chunk + 2 * (1 - x)
+        s_in(step).wait()
 
         @pl.loop(0, 4)
         def _(pair):
@@ -137,6 +154,8 @@
 
         a_copy(3 - step).start()
 
+    for operand in small_in:
+        operand.wait()
     base_row = 128 * jnp.clip(4 * first_quad // 128, 0, 4 * quad_count // 128 - 2)
     cols = sc_ref[:, pl.ds(pl.multiple_of(base_row, 128), 256)]
     want_at = lax.broadcasted_iota(jnp.int32, (4 * SPAN, 256), 0)
@@ -165,7 +184,7 @@
     codes[C_ROW : C_ROW + 8, :] = jnp.zeros((8, 256), jnp.int32)
     spot = ci_ref[...] - 4 * base_quad
     codes[C_ROW : C_ROW + 8, 0 : spot.shape[1]] = jnp.where((spot >= 0) & (spot < 4 * QUADS), spot, 4 * QUADS)
-    down_copy = pltpu.make_async_copy(codes, spots, in_sem.at[2])
+    down_copy = pltpu.make_async_copy(codes, spots, in_sem.at[8])
     down_copy.start()
 
     @pl.loop(0, 2 * QUADS + 1)
@@ -191,12 +210,15 @@
                     low16, l_table[spots[L_ROW + i, spot]], l_table[spots[L_ROW + i, spot + 1]]
                 )
 
-    def multiply(chunk, half):
+    def multiply(chunk, half, piece=None):
         view = chunk - skip
+        tiles = range(TILES) if piece is None else range(piece * PIECE, piece * PIECE + PIECE)
+        near_rows = range(8) if piece is None else range(4 * piece, 4 * piece + 4)
+        depth = slice(near_rows[0] * B, near_rows[-1] * B + B)
 
         @pl.loop(0, 2)
         def _(p):
-            for t in range(TILES):
+            for t in tiles:
                 v = near[chunk, 2 * half + p, t]
                 table[p * TILES + t] = v
                 table[40 + p * TILES + t] = swap(v)
@@ -205,68 +227,82 @@
         first = 4 * first_quad - base_row + view * 8
 
         for n in range(4):
-            for row in range(8):
+            for row in near_rows:
                 for w in range(2):
                     spot = 8 * n + 4 * w + 2 * half
                     dense_s[n, row * B : row * B + B, w * 128 : w * 128 + 128] = jnp.where(
                         low16, table[spots[spot, first + row]], table[spots[spot + 1, first + row]]
                     )
-            part = jnp.dot(dense_l[view], dense_s[n], preferred_element_type=jnp.float32)
+            part = jnp.dot(dense_l[view, :, depth], dense_s[n, depth, :], preferred_element_type=jnp.float32)
             at = 2 * (start + 2 * n) + half
             total[at] += part[:, :128]
             total[at + 2] += part[:, 128:]
 
-    events = ("A0", "A1", "X0", "C0", "A2", "X1", "C1", "A3", "E0", "X2", "X3", "E1")
+    events = ("A0", "A1", "X0", "C0", "A2", "X1", "C1", "A3", "E0", "X2")
 
     def when_prev(action):
         pl.when(has_prev)(action)
+
+    def used(order):
+        return jnp.where(outer, order != 0, order != 5) & (has_prev | (order < 4))
 
     def arrive_x(s):
         x_copy(s).wait_recv()
         if s < 2:
-            pl.when(has_next)(lambda: e_copy(s).start())
-            x_copy(s + 2).start()
+            for piece in pieces(s, 1):
+                pl.when(has_next)(lambda: e_copy(s, piece).start())
+                x_copy(s + 2, piece).start()
         d_copy(s).start()
 
     def arrive_c(s):
         c_copy(s).wait_recv()
         f_copy(s).start()
 
-    def arrive_e(s):
-        e_copy(s).wait_recv()
-        g_copy(s).start()
+    def arrive_e(s, piece=None):
+        e_copy(s, piece).wait_recv()
+        g_copy(s, piece).start()
 
     def before(kind, s):
         if kind == "A":
             a_copy(s).wait_recv()
         elif kind == "X":
-            if s != 2:
+            if s < 2:
                 arrive_x(s)
-                when_prev(lambda: arrive_e(1) if s == 3 else arrive_c(s))
+                when_prev(lambda: arrive_c(s))
             d_copy(s).wait_recv()
         elif kind == "C":
             when_prev(lambda: f_copy(s).wait_recv())
         else:
-            if s == 0:
-                when_prev(lambda: arrive_e(0))
-                arrive_x(2)
+            when_prev(lambda: arrive_e(s))
+            arrive_x(2)
             when_prev(lambda: g_copy(s).wait_recv())
 
     @pl.loop(0, len(events))
     def _(e):
-        order = e * 0
+        order, own_half = e * 0, e * 0
         for index, (kind, s) in enumerate(events):
             order = jnp.where(e == index, int(s) if kind in "AX" else 4 + int(s), order)
+            own_half = jnp.where(e == index, 1 if kind in "AC" else 0, own_half)
             pl.when(e == index)(functools.partial(before, kind, int(s)))
 
-        own_half = e * 0
-        for index, (kind, s) in enumerate(events):
-            own_half = jnp.where(e == index, 1 if kind in "AC" else 0, own_half)
-        halo = order >= 4
-
-        @pl.when(jnp.where(outer, order != 0, order != 5) & (has_prev | jnp.logical_not(halo)))
+        @pl.when(used(order))
         def _():
             multiply(flip(order), jnp.where(own_half == 1, x, 1 - x))
+
+    for piece in range(2):
+        x_copy(3, piece).wait_recv()
+        d_copy(3, piece).start()
+        when_prev(lambda: arrive_e(1, piece))
+
+        @pl.loop(0, 2)
+        def _(e):
+            pl.when(e == 0)(lambda: d_copy(3, piece).wait_recv())
+            pl.when((e == 1) & has_prev)(lambda: g_copy(1, piece).wait_recv())
+            order = 3 + 2 * e
+
+            @pl.when(used(order))
+            def _():
+                multiply(flip(order), 1 - x, piece)
 
     @pl.loop(0, 8)
     def _(i):
@@ -280,20 +316,23 @@
             out_ref[i, :, m * 128 : m * 128 + 128] = jnp.where(keep, straight, crossed).astype(jnp.bfloat16)
 
     for s in range(4):
-        x_copy(s).wait_send()
         a_copy(s).wait_send()
-        d_copy(s).wait_send()
+        for piece in pieces(s, 3):
+            x_copy(s, piece).wait_send()
+            d_copy(s, piece).wait_send()
     for s in range(2):
 
         @pl.when(has_next)
         def _():
             c_copy(s).wait_send()
-            e_copy(s).wait_send()
+            for piece in pieces(s, 1):
+                e_copy(s, piece).wait_send()
 
         @pl.when(has_prev)
         def _():
             f_copy(s).wait_send()
-            g_copy(s).wait_send()
+            for piece in pieces(s, 1):
+                g_copy(s, piece).wait_send()
 
 
 def shards(l_blocks, s_blocks, l_index, s_cols, c_index):
@@ -303,11 +342,14 @@
     return pl.pallas_call(
         functools.partial(kernel, row_count),
         out_shape=pltpu.VMEM((own, B, kept * B), jnp.bfloat16),
-        in_specs=[hbm, hbm, vmem, vmem, vmem],
+        in_specs=[hbm] * 5,
         out_specs=vmem,
         scratch_shapes=[
             pltpu.VMEM(s_blocks.shape, jnp.bfloat16),
             pltpu.VMEM(l_blocks.shape, jnp.bfloat16),
+            pltpu.VMEM(l_index.shape, jnp.int32),
+            pltpu.VMEM(s_cols.shape[::-1], jnp.int32),
+            pltpu.VMEM(c_index.shape, jnp.int32),
             pltpu.VMEM((CHUNKS, PARTS, TILES, B, 128), jnp.bfloat16),
             pltpu.VMEM((ZERO_S + 1, B, 128), jnp.bfloat16),
             pltpu.VMEM((4, 8 * B, 4 * B), jnp.bfloat16),
@@ -316,9 +358,9 @@
             pltpu.VMEM((2 * QUADS + 1, own * B, 128), jnp.float32),
             pltpu.VMEM((C_ROW + 8, 256), jnp.int32),
             pltpu.SMEM((C_ROW + 8, 256), jnp.int32),
-            pltpu.SemaphoreType.DMA((20,)),
-            pltpu.SemaphoreType.DMA((20,)),
-            pltpu.SemaphoreType.DMA((3,)),
+            pltpu.SemaphoreType.DMA((LATE + 5,)),
+            pltpu.SemaphoreType.DMA((LATE + 5,)),
+            pltpu.SemaphoreType.DMA((9,)),
         ],
         compiler_params=pltpu.CompilerParams(
             collective_id=0, has_side_effects=True, vmem_limit_bytes=56 * 1024 * 1024

time: 40.1 us -> 38.5 us (0.960); the launches traced: 39.4 us -> 38.4 us
  Pallas kernels: 38.3 us -> 37.2 us
    pallas_call x1, Pallas kernels: 38.3 us -> 37.2 us  [shards(): pl.pallas_call(functools.partial(kernel, row_count), out_shape=pltpu.VMEM...]
where the time goes in v6:
time: 38.5 us; the launch traced here: 38.4 us
  Pallas kernels  37.2 us (97%)
  local copies, waits for them, and re-layouts  1.15 us (3%)
    pallas_call x1, Pallas kernels, shards(): pl.pallas_call(functools.partial(kernel, row_count), out_shape=pltpu.VMEM...  37.2 us
    unnamed x1, local copies, waits for them, and re-layouts  1.15 us

profile of v6, /device:TPU:19, one launch (start us, length us, event | category | flops | bytes accessed | tf_op | source)
XLA Modules:
  0.0 38.4 jit_solution(1749770290608881670)
XLA Ops:
  0.0 37.2 %shard_map.55 = bf16[8,64,1536]{2,1,0:T(8,128)(2,1)S(1)} custom-call(bf16[32,64,320]{2,1,0:T(8,128)(2,1)} %s_hbm.1, bf16[8,64,1920]{2,1,0:T(8,128)(2,1)} %l_hbm.1, s32[8,30]{1,0:T(8,128)} %li_hbm.1, s32[20,256]{1,0:T(8,128)} %bitcast.1, s32[8,24]{1,0:T(8,128)} %ci_hbm.1), custom_call_target="tpu_custom_call" | custom-call | flops 4700000256 | bytes 5000000 | tf_op jit(solution)/shard_map/pallas_call | solution.py:342
  37.2 1.1 %copy.7 = bf16[8,64,1536]{2,1,0:T(8,128)(2,1)} copy(bf16[8,64,1536]{2,1,0:T(8,128)(2,1)S(1)} %shard_map.55) | data formatting | bytes 3145728

commit v7 on v6

--- a/solution.py
+++ b/solution.py
@@ -89,8 +89,13 @@
     def flip(t):
         return jnp.where(x == 1, t, 5 - t)
 
-    def copy(src_chunk, dst_chunk, part, index, device, piece=None):
-        tiles = slice(None) if piece is None else pl.ds(piece * PIECE, PIECE)
+    def copy(src_chunk, dst_chunk, part, index, device, piece=None, trim=False, near_quad=1 - x):
+        if piece is None:
+            tiles = pl.ds(2 * (1 - x), TILES - 2) if trim else slice(None)
+        elif piece == 0:
+            tiles = pl.ds(PIECE * near_quad, PIECE)
+        else:
+            tiles = pl.ds(2 + 8 * x, PIECE - 2) if trim else pl.ds(PIECE * (1 - near_quad), PIECE)
         index = index if not piece else LATE + (index - X0) // 4
         return pltpu.make_async_remote_copy(
             src_ref=near.at[src_chunk, part, tiles],
@@ -103,25 +108,25 @@
 
     def x_copy(s, piece=None):
         source, target = jnp.where(x == 0, s + 2, 3 - s), jnp.where(x == 0, s, 5 - s)
-        return copy(source, target, mine, X0 + s, across, piece)
+        return copy(source, target, mine, X0 + s, across, piece, near_quad=x)
 
     def a_copy(s):
         return copy(flip(s), flip(s), mine, A0 + s, core)
 
     def c_copy(s):
-        return copy(flip(s), flip(4 + s), mine, C0 + s, ahead)
+        return copy(flip(s), flip(4 + s), mine, C0 + s, ahead, trim=s == 1)
 
     def e_copy(s, piece=None):
-        return copy(flip(s), flip(4 + s), theirs, E0 + s, ahead, piece)
+        return copy(flip(s), flip(4 + s), theirs, E0 + s, ahead, piece, trim=s == 1)
 
     def d_copy(s, piece=None):
         return copy(flip(s), flip(s), theirs, D0 + s, core, piece)
 
     def f_copy(s):
-        return copy(flip(4 + s), flip(4 + s), mine, F0 + s, core)
+        return copy(flip(4 + s), flip(4 + s), mine, F0 + s, core, trim=s == 1)
 
     def g_copy(s, piece=None):
-        return copy(flip(4 + s), flip(4 + s), theirs, G0 + s, core, piece)
+        return copy(flip(4 + s), flip(4 + s), theirs, G0 + s, core, piece, trim=s == 1)
 
     def pieces(s, last):
         return (0, 1) if s == last else (None,)
@@ -137,8 +142,8 @@
             source = 8 * group_chunk + 2 * pair
             for odd in range(2):
                 for t in range(2):
-                    near[chunk, mine, at + 2 * odd + t] = s_ref[source + odd, :, t * 128 : t * 128 + 128]
-            near[chunk, mine, at + 4] = jnp.concatenate(
+                    near[chunk, mine, at + 3 * odd + t] = s_ref[source + odd, :, t * 128 : t * 128 + 128]
+            near[chunk, mine, at + 2] = jnp.concatenate(
                 [s_ref[source, :, 256:320], s_ref[source + 1, :, 256:320]], axis=1
             )
 
@@ -162,13 +167,14 @@
     row = lax.broadcasted_iota(jnp.int32, (4 * SPAN, 256), 1)
     odd, side = row % 2, want_at % 2
     want = 4 * jnp.clip(2 * ((base_row + row) // 8) - 3, 0, quad_count - SPAN) + want_at
+    want = jnp.where(base_row + row == 32 * r + jnp.where(x == 0, -16, 47), -1, want)
     first_tile = ((row // 2) % 4) * 5
     code = jnp.full((4 * SPAN, 256), ZERO_S, jnp.int32)
     for within in range(KSP):
         if within < 4:
-            tile = first_tile + 2 * odd + within // 2 + jnp.where(side != within % 2, 40, 0)
+            tile = first_tile + 3 * odd + within // 2 + jnp.where(side != within % 2, 40, 0)
         else:
-            tile = first_tile + 4 + jnp.where(side != odd, 40, 0)
+            tile = first_tile + 2 + jnp.where(side != odd, 40, 0)
         for part in range(PARTS):
             slot = part * KSP + within
             code = jnp.where(cols[slot : slot + 1, :] == want, tile + (part % 2) * TILES, code)
@@ -210,30 +216,35 @@
                     low16, l_table[spots[L_ROW + i, spot]], l_table[spots[L_ROW + i, spot + 1]]
                 )
 
-    def multiply(chunk, half, piece=None):
+    def multiply(chunk, half, quad=None):
         view = chunk - skip
-        tiles = range(TILES) if piece is None else range(piece * PIECE, piece * PIECE + PIECE)
-        near_rows = range(8) if piece is None else range(4 * piece, 4 * piece + 4)
-        depth = slice(near_rows[0] * B, near_rows[-1] * B + B)
+        if quad is None:
+            near_rows, tile_count, tile_first = 8, TILES, 0
+            left = dense_l.at[view]
+        else:
+            near_rows, tile_count, tile_first = 4, PIECE, PIECE * quad
+            left = dense_l.at[view, :, pl.ds(pl.multiple_of(4 * B * quad, 4 * B), 4 * B)]
+        depth = slice(0, near_rows * B)
 
         @pl.loop(0, 2)
         def _(p):
-            for t in tiles:
-                v = near[chunk, 2 * half + p, t]
-                table[p * TILES + t] = v
-                table[40 + p * TILES + t] = swap(v)
+            for t in range(tile_count):
+                at = tile_first + t
+                v = near[chunk, 2 * half + p, at]
+                table[p * TILES + at] = v
+                table[40 + p * TILES + at] = swap(v)
 
         start = jnp.clip(first_quad + 2 * view - 3, 0, quad_count - SPAN) - base_quad
-        first = 4 * first_quad - base_row + view * 8
+        first = 4 * first_quad - base_row + view * 8 + (0 if quad is None else 4 * quad)
 
         for n in range(4):
-            for row in near_rows:
+            for row in range(near_rows):
                 for w in range(2):
                     spot = 8 * n + 4 * w + 2 * half
                     dense_s[n, row * B : row * B + B, w * 128 : w * 128 + 128] = jnp.where(
                         low16, table[spots[spot, first + row]], table[spots[spot + 1, first + row]]
                     )
-            part = jnp.dot(dense_l[view, :, depth], dense_s[n, depth, :], preferred_element_type=jnp.float32)
+            part = jnp.dot(left[...], dense_s[n, depth, :], preferred_element_type=jnp.float32)
             at = 2 * (start + 2 * n) + half
             total[at] += part[:, :128]
             total[at + 2] += part[:, 128:]
@@ -289,6 +300,22 @@
         def _():
             multiply(flip(order), jnp.where(own_half == 1, x, 1 - x))
 
+    def pick(half):
+        @pl.loop(0, 8)
+        def _(i):
+            rows = pl.ds(pl.multiple_of(i * B, B), B)
+            for m in range(6):
+                slot = 12 * half + 2 * m
+                left, right = spots[C_ROW + i, slot], spots[C_ROW + i, slot + 1]
+                a, b = total[left // 2, rows, :], total[right // 2, rows, :]
+                straight = jnp.where(low, a, b)
+                crossed = pltpu.roll(jnp.where(low, b, a), B, 1)
+                keep = jnp.where(low, 1 - left % 2, right % 2) == 1
+                at = pl.ds(pl.multiple_of(slot * B, 2 * B), 2 * B)
+                out_ref[i, :, at] = jnp.where(keep, straight, crossed).astype(jnp.bfloat16)
+
+    pick(x)
+
     for piece in range(2):
         x_copy(3, piece).wait_recv()
         d_copy(3, piece).start()
@@ -302,18 +329,9 @@
 
             @pl.when(used(order))
             def _():
-                multiply(flip(order), 1 - x, piece)
-
-    @pl.loop(0, 8)
-    def _(i):
-        rows = pl.ds(pl.multiple_of(i * B, B), B)
-        for m in range(12):
-            left, right = spots[C_ROW + i, 2 * m], spots[C_ROW + i, 2 * m + 1]
-            a, b = total[left // 2, rows, :], total[right // 2, rows, :]
-            straight = jnp.where(low, a, b)
-            crossed = pltpu.roll(jnp.where(low, b, a), B, 1)
-            keep = jnp.where(low, 1 - left % 2, right % 2) == 1
-            out_ref[i, :, m * 128 : m * 128 + 128] = jnp.where(keep, straight, crossed).astype(jnp.bfloat16)
+                multiply(flip(order), 1 - x, 1 - x if piece == 0 else x)
+
+    pick(1 - x)
 
     for s in range(4):
         a_copy(s).wait_send()

time: 38.5 us -> 38.8 us (level)
  no operation moved by 1% of the time
where the time goes in v7:
time: 38.8 us; the launch traced here: 38.6 us
  Pallas kernels  37.5 us (97%)
  local copies, waits for them, and re-layouts  1.15 us (3%)
    pallas_call x1, Pallas kernels, shards(): pl.pallas_call(functools.partial(kernel, row_count), out_shape=pltpu.VMEM...  37.5 us
    unnamed x1, local copies, waits for them, and re-layouts  1.15 us

profile of v7, /device:TPU:19, one launch (start us, length us, event | category | flops | bytes accessed | tf_op | source)
XLA Modules:
  0.0 38.6 jit_solution(6320882299061761965)
XLA Ops:
  0.0 37.5 %shard_map.55 = bf16[8,64,1536]{2,1,0:T(8,128)(2,1)S(1)} custom-call(bf16[32,64,320]{2,1,0:T(8,128)(2,1)} %s_hbm.1, bf16[8,64,1920]{2,1,0:T(8,128)(2,1)} %l_hbm.1, s32[8,30]{1,0:T(8,128)} %li_hbm.1, s32[20,256]{1,0:T(8,128)} %bitcast.1, s32[8,24]{1,0:T(8,128)} %ci_hbm.1), custom_call_target="tpu_custom_call" | custom-call | flops 4700000256 | bytes 5000000 | tf_op jit(solution)/shard_map/pallas_call | solution.py:360
  37.5 1.1 %copy.7 = bf16[8,64,1536]{2,1,0:T(8,128)(2,1)} copy(bf16[8,64,1536]{2,1,0:T(8,128)(2,1)S(1)} %shard_map.55) | data formatting | bytes 3145728

commit v8 on v7

--- a/solution.py
+++ b/solution.py
@@ -52,6 +52,8 @@
     core = (r, 2 * x + 1 - k)
     across = (r, 2 * (1 - x) + k)
     ahead = (next_row, c)
+    ahead_outer = (next_row, 3 * x)
+    outer_core = k == x
     mine, theirs = c, 2 * (1 - x) + k
     quad_count = 8 * row_count
     base_quad = jnp.clip(first_quad - 3, 0, quad_count - QUADS)
@@ -63,10 +65,12 @@
     @pl.when(up)
     def _():
         pl.semaphore_signal(barrier, inc=1, device_id=(r + 1, c), device_id_type=MESH)
+        pl.semaphore_signal(barrier, inc=1, device_id=(r + 1, 2 * x + 1 - k), device_id_type=MESH)
 
     @pl.when(down)
     def _():
         pl.semaphore_signal(barrier, inc=1, device_id=(r - 1, c), device_id_type=MESH)
+        pl.semaphore_signal(barrier, inc=1, device_id=(r - 1, 2 * x + 1 - k), device_id_type=MESH)
 
     def s_in(step):
         rows = pl.ds(8 * jnp.where(x == 0, step, 3 - step), 8)
@@ -96,7 +100,7 @@
             tiles = pl.ds(PIECE * near_quad, PIECE)
         else:
             tiles = pl.ds(2 + 8 * x, PIECE - 2) if trim else pl.ds(PIECE * (1 - near_quad), PIECE)
-        index = index if not piece else LATE + (index - X0) // 4
+        index = LATE + (index - X0) // 4 if piece else index
         return pltpu.make_async_remote_copy(
             src_ref=near.at[src_chunk, part, tiles],
             dst_ref=near.at[dst_chunk, part, tiles],
@@ -114,10 +118,15 @@
         return copy(flip(s), flip(s), mine, A0 + s, core)
 
     def c_copy(s):
-        return copy(flip(s), flip(4 + s), mine, C0 + s, ahead, trim=s == 1)
+        if s == 1:
+            return copy(flip(1), flip(5), mine, jnp.where(outer_core, C0 + 1, F0 + 1), ahead_outer, trim=True)
+        return copy(flip(s), flip(4 + s), mine, C0 + s, ahead)
 
     def e_copy(s, piece=None):
-        return copy(flip(s), flip(4 + s), theirs, E0 + s, ahead, piece, trim=s == 1)
+        if s == 1:
+            index = jnp.where(outer_core, E0 + 1, G0 + 1)
+            return copy(flip(1), flip(5), theirs, index, ahead_outer, piece, trim=True)
+        return copy(flip(s), flip(4 + s), theirs, E0 + s, ahead)
 
     def d_copy(s, piece=None):
         return copy(flip(s), flip(s), theirs, D0 + s, core, piece)
@@ -148,7 +157,7 @@
             )
 
         if step == 0:
-            pl.semaphore_wait(barrier, 2 + up.astype(jnp.int32) + down.astype(jnp.int32))
+            pl.semaphore_wait(barrier, 2 + 2 * up.astype(jnp.int32) + 2 * down.astype(jnp.int32))
         if step < 2:
             x_copy(step).start()
         else:
@@ -269,9 +278,9 @@
         c_copy(s).wait_recv()
         f_copy(s).start()
 
-    def arrive_e(s, piece=None):
-        e_copy(s, piece).wait_recv()
-        g_copy(s, piece).start()
+    def arrive_e(s):
+        e_copy(s).wait_recv()
+        g_copy(s).start()
 
     def before(kind, s):
         if kind == "A":
@@ -279,10 +288,19 @@
         elif kind == "X":
             if s < 2:
                 arrive_x(s)
-                when_prev(lambda: arrive_c(s))
+                if s == 0:
+                    when_prev(lambda: arrive_c(0))
             d_copy(s).wait_recv()
         elif kind == "C":
-            when_prev(lambda: f_copy(s).wait_recv())
+            if s == 0:
+                when_prev(lambda: f_copy(0).wait_recv())
+            else:
+
+                @pl.when(has_prev & outer_core)
+                def _():
+                    c_copy(1).wait_recv()
+                    f_copy(1).wait_recv()
+
         else:
             when_prev(lambda: arrive_e(s))
             arrive_x(2)
@@ -319,13 +337,16 @@
     for piece in range(2):
         x_copy(3, piece).wait_recv()
         d_copy(3, piece).start()
-        when_prev(lambda: arrive_e(1, piece))
+
+        def halo_piece():
+            e_copy(1, piece).wait_recv()
+            g_copy(1, piece).wait_recv()
 
         @pl.loop(0, 2)
         def _(e):
-            pl.when(e == 0)(lambda: d_copy(3, piece).wait_recv())
-            pl.when((e == 1) & has_prev)(lambda: g_copy(1, piece).wait_recv())
-            order = 3 + 2 * e
+            pl.when((e == 0) & has_prev & outer_core)(halo_piece)
+            pl.when(e == 1)(lambda: d_copy(3, piece).wait_recv())
+            order = 5 - 2 * e
 
             @pl.when(used(order))
             def _():
@@ -348,9 +369,9 @@
 
         @pl.when(has_prev)
         def _():
-            f_copy(s).wait_send()
-            for piece in pieces(s, 1):
-                g_copy(s, piece).wait_send()
+            if s == 0:
+                f_copy(s).wait_send()
+                g_copy(s).wait_send()
 
 
 def shards(l_blocks, s_blocks, l_index, s_cols, c_index):

time: 38.8 us -> 38.4 us (0.990); the launches traced: 38.6 us -> 37.7 us
  Pallas kernels: 37.5 us -> 36.6 us
    pallas_call x1, Pallas kernels: 37.5 us -> 36.6 us  [shards(): pl.pallas_call(functools.partial(kernel, row_count), out_shape=pltpu.VMEM...]
where the time goes in v8:
time: 38.4 us; the launch traced here: 37.7 us
  Pallas kernels  36.6 us (95%)
  local copies, waits for them, and re-layouts  1.15 us (3%)
    pallas_call x1, Pallas kernels, shards(): pl.pallas_call(functools.partial(kernel, row_count), out_shape=pltpu.VMEM...  36.6 us
    unnamed x1, local copies, waits for them, and re-layouts  1.15 us

profile of v8, /device:TPU:19, one launch (start us, length us, event | category | flops | bytes accessed | tf_op | source)
XLA Modules:
  0.0 37.7 jit_solution(12716204375717573527)
XLA Ops:
  0.0 36.6 %shard_map.55 = bf16[8,64,1536]{2,1,0:T(8,128)(2,1)S(1)} custom-call(bf16[32,64,320]{2,1,0:T(8,128)(2,1)} %s_hbm.1, bf16[8,64,1920]{2,1,0:T(8,128)(2,1)} %l_hbm.1, s32[8,30]{1,0:T(8,128)} %li_hbm.1, s32[20,256]{1,0:T(8,128)} %bitcast.1, s32[8,24]{1,0:T(8,128)} %ci_hbm.1), custom_call_target="tpu_custom_call" | custom-call | flops 4700000256 | bytes 5000000 | tf_op jit(solution)/shard_map/pallas_call | solution.py:381
  36.6 1.1 %copy.7 = bf16[8,64,1536]{2,1,0:T(8,128)(2,1)} copy(bf16[8,64,1536]{2,1,0:T(8,128)(2,1)S(1)} %shard_map.55) | data formatting | bytes 3145728

commit v9 on v8

--- a/solution.py
+++ b/solution.py
@@ -258,7 +258,7 @@
             total[at] += part[:, :128]
             total[at + 2] += part[:, 128:]
 
-    events = ("A0", "A1", "X0", "C0", "A2", "X1", "C1", "A3", "E0", "X2")
+    events = ("A0", "A1", "A2", "X0", "C0", "A3", "X1", "C1", "E0", "X2")
 
     def when_prev(action):
         pl.when(has_prev)(action)
@@ -332,8 +332,6 @@
                 at = pl.ds(pl.multiple_of(slot * B, 2 * B), 2 * B)
                 out_ref[i, :, at] = jnp.where(keep, straight, crossed).astype(jnp.bfloat16)
 
-    pick(x)
-
     for piece in range(2):
         x_copy(3, piece).wait_recv()
         d_copy(3, piece).start()
@@ -352,7 +350,7 @@
             def _():
                 multiply(flip(order), 1 - x, 1 - x if piece == 0 else x)
 
-    pick(1 - x)
+        pick(x if piece == 0 else 1 - x)
 
     for s in range(4):
         a_copy(s).wait_send()

time: 38.4 us -> 38.8 us (1.010)
  the two profiles are of different devices: /device:TPU:19 before, /device:TPU:0 now
where the time goes in v9:
time: 38.8 us; the launch traced here: 38.7 us
  Pallas kernels  37.5 us (97%)
  local copies, waits for them, and re-layouts  1.15 us (3%)
    pallas_call x1, Pallas kernels, shards(): pl.pallas_call(functools.partial(kernel, row_count), out_shape=pltpu.VMEM...  37.5 us
    unnamed x1, local copies, waits for them, and re-layouts  1.15 us

profile of v9, /device:TPU:0, one launch (start us, length us, event | category | flops | bytes accessed | tf_op | source)
XLA Modules:
  0.0 38.7 jit_solution(18270386691989926460)
XLA Ops:
  0.0 37.5 %shard_map.55 = bf16[8,64,1536]{2,1,0:T(8,128)(2,1)S(1)} custom-call(bf16[32,64,320]{2,1,0:T(8,128)(2,1)} %s_hbm.1, bf16[8,64,1920]{2,1,0:T(8,128)(2,1)} %l_hbm.1, s32[8,30]{1,0:T(8,128)} %li_hbm.1, s32[20,256]{1,0:T(8,128)} %bitcast.1, s32[8,24]{1,0:T(8,128)} %ci_hbm.1), custom_call_target="tpu_custom_call" | custom-call | flops 4700000256 | bytes 5000000 | tf_op jit(solution)/shard_map/pallas_call | solution.py:379
  37.5 1.1 %copy.7 = bf16[8,64,1536]{2,1,0:T(8,128)(2,1)} copy(bf16[8,64,1536]{2,1,0:T(8,128)(2,1)S(1)} %shard_map.55) | data formatting | bytes 3145728
